TPU v7x, 32 devices: a whole 2x2x4 slice. The times are simulated.
32 devices in a mesh: prow: 4 (over z), pcol: 8 (over y, x, core).
Axes of the slice: x: 2, y: 2, z: 4, core: 2. Of those that a mesh axis runs over, the one named last changes fastest.
Arguments:
- matrix: bfloat16 [8, 4, 5, 8, 256, 256], P(None, 'prow', None, 'pcol'), may hold values from -6 to 6
- lower_inverse: bfloat16 [4, 256, 256], replicated
- upper_inverse: bfloat16 [4, 256, 256], replicated
- row_first: int32 [8, 4], P(None, 'prow'), may hold values from 0 to 4, as said below
- col_mask: int32 [4, 5, 8], P(None, None, 'pcol'), may hold values from 0 to 1, as said below
Outputs:
- factored: bfloat16 [8, 4, 5, 8, 256, 256], P(None, 'prow', None, 'pcol')
Inputs may be any that keep to these rules, and one draw needn't show every extreme that they name: `row_first`: 4 means no panel; tile rows below 4 take 4. `col_mask`: 0 for tile columns j <= k, 1 for k < j < 4.
All inputs are finite; a program needn't handle non-finite values.
Results may differ from a plain program's by a relative error of at most 0.007.
Values may be sent and summed in bfloat16 or wider, within the bound.
No kernel may reach another device: no remote copies, remote signals or barrier semaphores. Data moves between devices by JAX's collectives and lax.ppermute only.
A program may use at most 128 MiB of HBM per device.

v0:
```python
import jax
import jax.numpy as jnp
from jax import lax
from jax.sharding import PartitionSpec as P


def spread(block, axis, owner):
    block = jnp.where(lax.axis_index(axis) == owner, block, jnp.zeros_like(block))
    return lax.psum(block, axis)


def solve_lower(column, inverse, row_live):
    solved = jnp.einsum(
        "rab,bc->rac", column, inverse.astype(jnp.float32), precision=lax.Precision.HIGHEST
    )
    return jnp.where(row_live[:, None, None], solved, 0.0).astype(jnp.bfloat16)


def solve_upper(row_tiles, inverse, col_live):
    solved = jnp.einsum("ab,jbc->jac", inverse, row_tiles, preferred_element_type=jnp.float32)
    return jnp.where(col_live[:, None, None], solved, 0.0).astype(jnp.bfloat16)


def apply_update(block, lower_panel, upper_panel, row_live):

    def update_row(triple):
        tile_row, lower_tile, active = triple
        return lax.cond(
            active,
            lambda: tile_row
            - jnp.einsum(
                "ab,jbc->jac", lower_tile, upper_panel, preferred_element_type=jnp.float32
            ),
            lambda: tile_row,
        )

    return lax.map(update_row, (block, lower_panel, row_live))


def local(matrix, lower_inverse, upper_inverse, row_first, col_mask):
    local_rows = matrix.shape[0]
    local_cols = matrix.shape[2]
    tile_size = matrix.shape[4]
    panels = lower_inverse.shape[0]
    tile_grid = matrix.reshape(local_rows, local_cols, tile_size, tile_size)
    running = tile_grid.astype(jnp.float32)
    first_flat = row_first.reshape(local_rows)
    col_flat = col_mask.reshape(panels, local_cols)
    prow_at = lax.axis_index("prow")
    pcol_at = lax.axis_index("pcol")
    column = running[:, 0]
    lowers = []
    uppers = []
    for panel in range(panels):
        row_live = first_flat <= panel
        col_live = col_flat[panel] == 1
        lower_mine = lax.cond(
            pcol_at == panel,
            lambda: solve_lower(column, upper_inverse[panel], row_live),
            lambda: jnp.zeros((local_rows, tile_size, tile_size), jnp.bfloat16),
        )
        lower_panel = spread(lower_mine, "pcol", panel)
        upper_mine = lax.cond(
            prow_at == panel,
            lambda: solve_upper(tile_grid[0], lower_inverse[panel], col_live),
            lambda: jnp.zeros((local_cols, tile_size, tile_size), jnp.bfloat16),
        )
        upper_panel = spread(upper_mine, "prow", panel)
        column = apply_update(running[:, :1], lower_panel, upper_panel[:1], row_live)[:, 0]
        remainder = apply_update(running[:, 1:], lower_panel, upper_panel[1:], row_live)
        running = jnp.concatenate([column[:, None], remainder], axis=1)
        lowers.append(lower_panel)
        uppers.append(upper_panel)
    result = running.astype(jnp.bfloat16)
    lower_pick = jnp.stack(lowers)[jnp.clip(pcol_at, 0, panels - 1)]
    result = result.at[:, 0].set(jnp.where(pcol_at < panels, lower_pick, result[:, 0]))
    upper_pick = jnp.stack(uppers)[jnp.clip(prow_at, 0, panels - 1)]
    result = result.at[0].set(jnp.where(prow_at < panels, upper_pick, result[0]))
    return result.reshape(local_rows, 1, local_cols, 1, tile_size, tile_size)


def solution(mesh):
    return jax.shard_map(
        local,
        mesh=mesh,
        in_specs=(
            P(None, "prow", None, "pcol", None, None),
            P(),
            P(),
            P(None, "prow"),
            P(None, None, "pcol"),
        ),
        out_specs=P(None, "prow", None, "pcol", None, None),
        check_vma=False,
    )
```

profile of v0, /device:TPU:0, one launch (start us, length us, event | category | flops | bytes accessed | tf_op | source)
XLA Modules:
  0.0 518.1 jit_solution(8446088891613646111)
XLA Ops:
  6.5 7.8 %copy.7 = bf16[8,5,256,256]{2,3,1,0:T(8,128)(2,1)} copy(bf16[8,5,256,256]{3,2,1,0:T(8,128)(2,1)} %bitcast.310) | data formatting | bytes 10485760 | tf_op jit(solution)/shard_map/cond | solution.py:63
  15.4 1.7 conditional.17
  15.4 1.5 fusion.7
  19.4 3.8 bitcast_convert_fusion
  23.2 4.0 copy-done
  27.3 1.6 slice.155
  28.9 2.7 conditional.16
  28.9 2.7 select_convert_fusion
  32.7 7.6 %slice.160 = f32[8,4,256,256]{3,2,1,0:T(8,128)} slice(f32[8,5,256,256]{3,2,1,0:T(8,128)} %copy-done), slice={[0:8], [1:5], [0:256], [0:256]} | slice | bytes 16777216 | tf_op jit(solution)/shard_map/slice | solution.py:70
  41.4 2.5 broadcast_convert_fusion
  43.9 83.5 %all-reduce.15.cloned.1.call-done = (bf16[5,256,256]{2,1,0:T(8,128)(2,1)}, bf16[5,256,256]{2,1,0:T(8,128)(2,1)}, bf16[5,256,256]{2,1,0:T(8,128)(2,1)}, bf16[5,256,256]{2,1,0:T(8,128)(2,1)}) async-done(((bf16[5,256,256]{2,1,0:T(8,128)(2,1)}, bf16[5,256,256]{2,1,0:T(8,128)(2,1)}, bf16[5,256,256]{2,1,0:T(8,128)(2,1)}, bf16[5,256,256]{2,1,0:T(8,128)(2,1)}), (bf16[5,256,256]{2,1,0:T(8,128)(2,1)}, ...) | async-done | bytes 2621456 | tf_op jit(solution)/shard_map/psum | solution.py:9
  129.4 56.7 %all-reduce.7.cloned.1.call-done = bf16[8,256,256]{2,1,0:T(8,128)(2,1)} async-done(((bf16[8,256,256]{2,1,0:T(8,128)(2,1)}), bf16[8,256,256]{2,1,0:T(8,128)(2,1)}) %all-reduce.7.cloned.1.call-update) | async-done | bytes 1048592 | tf_op jit(solution)/shard_map/psum | solution.py:9
  186.1 1.5 broadcast.139.clone
  187.6 26.4 %while.82 = (s32[]{:T(128)}, f32[8,1,256,256]{3,2,1,0:T(8,128)}, pred[8]{0:T(512)(128)(4,1)S(1)}, f32[8,1,256,256]{3,2,1,0:T(8,128)}, bf16[8,256,256]{2,1,0:T(8,...) while((s32[]{:T(128)}, f32[8,1,256,256]{3,2,1,0:T(8,128)}, pred[8]{0:T(512)(128)(4,1)S(1)}, ...), condition=%wide.region_9.10_spmd, body=%wide.region_6.9_spmd.sunk | while | flops 33619968 | bytes 1836164 | solution.py:37
  215.3 4.3 broadcast.147.clone.1
  219.5 31.0 %while.86 = (s32[]{:T(128)}, f32[8,4,256,256]{3,2,1,0:T(8,128)}, pred[8]{0:T(512)(128)(4,1)S(1)}, f32[8,4,256,256]{3,2,1,0:T(8,128)}, bf16[8,256,256]{2,1,0:T(8,...) while((s32[]{:T(128)}, f32[8,4,256,256]{3,2,1,0:T(8,128)}, pred[8]{0:T(512)(128)(4,1)S(1)}, ...), condition=%wide.region_43.44_spmd, body=%wide.region_40.43_spmd.sunk | while | flops 134479872 | bytes 6947972 | solution.py:37
  252.8 18.3 %all-reduce.9.cloned.1.call-done = bf16[8,256,256]{2,1,0:T(8,128)(2,1)} async-done(((bf16[8,256,256]{2,1,0:T(8,128)(2,1)}), bf16[8,256,256]{2,1,0:T(8,128)(2,1)}) %all-reduce.9.cloned.1.call-update) | async-done | bytes 1048592 | tf_op jit(solution)/shard_map/psum | solution.py:9
  271.1 1.6 broadcast.139.clone.1
  272.7 25.2 %while.83 = (s32[]{:T(128)}, f32[8,1,256,256]{3,2,1,0:T(8,128)}, pred[8]{0:T(512)(128)(4,1)S(1)}, f32[8,1,256,256]{3,2,1,0:T(8,128)}, bf16[8,256,256]{2,1,0:T(8,...) while((s32[]{:T(128)}, f32[8,1,256,256]{3,2,1,0:T(8,128)}, pred[8]{0:T(512)(128)(4,1)S(1)}, ...), condition=%wide.region_19.20_spmd, body=%wide.region_16.19_spmd.sunk | while | flops 33619968 | bytes 1836164 | solution.py:37
  299.3 4.3 broadcast.147.clone
  303.5 32.4 %while.87 = (s32[]{:T(128)}, f32[8,4,256,256]{3,2,1,0:T(8,128)}, pred[8]{0:T(512)(128)(4,1)S(1)}, f32[8,4,256,256]{3,2,1,0:T(8,128)}, bf16[8,256,256]{2,1,0:T(8,...) while((s32[]{:T(128)}, f32[8,4,256,256]{3,2,1,0:T(8,128)}, pred[8]{0:T(512)(128)(4,1)S(1)}, ...), condition=%wide.region_47.48_spmd, body=%wide.region_44.47_spmd.sunk | while | flops 134479872 | bytes 6947972 | solution.py:37
  335.9 23.8 %all-reduce.11.cloned.1.call-done = bf16[8,256,256]{2,1,0:T(8,128)(2,1)} async-done(((bf16[8,256,256]{2,1,0:T(8,128)(2,1)}), bf16[8,256,256]{2,1,0:T(8,128)(2,1)}) %all-reduce.11.cloned.1.call-update) | async-done | bytes 1048592 | tf_op jit(solution)/shard_map/psum | solution.py:9
  359.7 1.5 broadcast.139
  361.2 25.2 %while.84 = (s32[]{:T(128)}, f32[8,1,256,256]{3,2,1,0:T(8,128)}, pred[8]{0:T(512)(128)(4,1)S(1)}, f32[8,1,256,256]{3,2,1,0:T(8,128)}, bf16[8,256,256]{2,1,0:T(8,...) while((s32[]{:T(128)}, f32[8,1,256,256]{3,2,1,0:T(8,128)}, pred[8]{0:T(512)(128)(4,1)S(1)}, ...), condition=%wide.region_29.30_spmd, body=%wide.region_26.29_spmd.sunk | while | flops 33619968 | bytes 1836164 | solution.py:37
  387.6 4.3 broadcast.147
  391.8 31.0 %while.88 = (s32[]{:T(128)}, f32[8,4,256,256]{3,2,1,0:T(8,128)}, pred[8]{0:T(512)(128)(4,1)S(1)}, f32[8,4,256,256]{3,2,1,0:T(8,128)}, bf16[8,256,256]{2,1,0:T(8,...) while((s32[]{:T(128)}, f32[8,4,256,256]{3,2,1,0:T(8,128)}, pred[8]{0:T(512)(128)(4,1)S(1)}, ...), condition=%wide.region_51.52_spmd, body=%wide.region_48.51_spmd.sunk | while | flops 134479872 | bytes 6947972 | solution.py:37
  422.9 23.7 %all-reduce.13.cloned.1.call-done = bf16[8,256,256]{2,1,0:T(8,128)(2,1)} async-done(((bf16[8,256,256]{2,1,0:T(8,128)(2,1)}), bf16[8,256,256]{2,1,0:T(8,128)(2,1)}) %all-reduce.13.cloned.1.call-update) | async-done | bytes 1048592 | tf_op jit(solution)/shard_map/psum | solution.py:9
  446.5 23.0 %while.85 = (s32[]{:T(128)}, bf16[8,1,256,256]{3,2,1,0:T(8,128)(2,1)S(1)}, pred[8]{0:T(512)(128)(4,1)S(1)}, f32[8,1,256,256]{3,2,1,0:T(8,128)}, bf16[8,256,256]{...) while((s32[]{:T(128)}, bf16[8,1,256,256]{3,2,1,0:T(8,128)(2,1)S(1)}, ...), condition=%wide.region_39.40_spmd, body=%wide.region_36.39_spmd.sunk | while | flops 33619968 | bytes 1835656 | solution.py:37
  469.5 32.6 %while.89 = (s32[]{:T(128)}, bf16[8,4,256,256]{3,2,1,0:T(8,128)(2,1)}, pred[8]{0:T(512)(128)(4,1)S(1)}, f32[8,4,256,256]{3,2,1,0:T(8,128)}, bf16[8,256,256]{2,1,...) while((s32[]{:T(128)}, bf16[8,4,256,256]{3,2,1,0:T(8,128)(2,1)}, pred[8]{0:T(512)(128)(4,1)S(1)}, ...), condition=%wide.region_55.56_spmd, body=%wide.region_52.55_spmd.sunk | while | flops 134479872 | bytes 6947972 | solution.py:37
  502.1 2.8 pad_maximum_fusion
  506.6 2.6 copy.124
  510.1 1.4 bitcast_dynamic-update-slice_fusion
  (350 shorter events, 226.8 us)
Async XLA Ops:
  6.5 120.8 %all-reduce.15.cloned.1.call-start = ((), (), s32[]{:S(2)}) async-start(), calls=%async_computation.4 | async-start | bytes 5242880 | tf_op jit(solution)/shard_map/psum | solution.py:9
  6.5 7.8 %copy-start.14 = (bf16[4,256,256]{2,1,0:T(8,128)(2,1)S(1)}, bf16[4,256,256]{2,1,0:T(8,128)(2,1)}, u32[]{:S(2)}) copy-start(bf16[4,256,256]{2,1,0:T(8,128)(2,1)} %param.58) | copy-start | bytes 1572868
  6.5 7.8 %copy-start.15 = (s32[4,5,1]{1,2,0:T(1,128)S(1)}, s32[4,5,1]{1,2,0:T(1,128)}, u32[]{:S(2)}) copy-start(s32[4,5,1]{1,2,0:T(1,128)} %param.61) | copy-start | bytes 244
  19.4 166.8 %all-reduce.7.cloned.1.call-start = ((), (), s32[]{:S(2)}) async-start(), calls=%async_computation | async-start | bytes 2097152 | tf_op jit(solution)/shard_map/psum | solution.py:9
  23.2 4.0 copy-start
  27.3 1.6 copy-start.13
  27.3 1.6 copy-start.12
  32.7 238.5 %all-reduce.9.cloned.1.call-start = ((), (), s32[]{:S(2)}) async-start(), calls=%async_computation.1 | async-start | bytes 2097152 | tf_op jit(solution)/shard_map/psum | solution.py:9
  215.2 144.5 %all-reduce.11.cloned.1.call-start = ((), (), s32[]{:S(2)}) async-start(), calls=%async_computation.2 | async-start | bytes 2097152 | tf_op jit(solution)/shard_map/psum | solution.py:9
  219.5 31.1 %copy-start.7 = (bf16[5,256,256]{2,1,0:T(8,128)(2,1)S(1)}, bf16[5,256,256]{2,1,0:T(8,128)(2,1)}, u32[]{:S(2)}) copy-start(bf16[5,256,256]{2,1,0:T(8,128)(2,1)} %get-tuple-element.818) | copy-start | bytes 1966084
  250.6 2.1 copy-start.10
  299.0 147.5 %all-reduce.13.cloned.1.call-start = ((), (), s32[]{:S(2)}) async-start(), calls=%async_computation.3 | async-start | bytes 2097152 | tf_op jit(solution)/shard_map/psum | solution.py:9
  391.8 54.7 %copy-start.1 = (bf16[8,1,256,256]{3,2,1,0:T(8,128)(2,1)S(1)}, bf16[8,1,256,256]{3,2,1,0:T(8,128)(2,1)}, u32[]{:S(2)}) copy-start(bf16[8,1,256,256]{3,2,1,0:T(8,128)(2,1)} %broadcast_convert_fusion.1) | copy-start | bytes 3145732
  502.1 2.8 copy-start.2
  502.1 2.8 copy-start.3
  502.1 3.1 copy-start.4
  502.1 3.4 copy-start.5
  506.6 2.7 copy-start.6
  506.6 2.7 copy-start.8
  506.6 2.8 copy-start.9
  506.6 3.5 copy-start.11
Sparse Core Ops, SparseCore 0:
  19.5 107.8 all-reduce.14
  130.5 55.5 all-reduce.6
  215.3 55.7 all-reduce.8
  299.2 60.4 all-reduce.10
  387.7 58.8 all-reduce.12
where the time goes:
time: 527 us; the launch traced here: 518 us
  local copies, waits for them, and re-layouts  210 us (40%)
  waiting for transfers between devices  206 us (39%)
  loops' own time  40.6 us (8%)
  matrix products  27.5 us (5%)
  other arithmetic  19.9 us (4%)
  between operations  13.4 us (3%)
    psum x5, waiting for transfers between devices, spread(): return lax.psum(block, axis)  206 us
    squeeze x64, local copies, waits for them, and re-layouts, apply_update(): return lax.map(update_row, (block, lower_panel, row_live))  72.9 us
    dynamic_update_slice x64, local copies, waits for them, and re-layouts, apply_update(): return lax.map(update_row, (block, lower_panel, row_live))  50.2 us
    another operation x8, loops' own time, apply_update(): return lax.map(update_row, (block, lower_panel, row_live))  39.9 us
    dynamic_slice x64, local copies, waits for them, and re-layouts, apply_update(): return lax.map(update_row, (block, lower_panel, row_live))  39.8 us
    dot_general x20, matrix products, update_row(): jnp.einsum('ab,jbc->jac', lower_tile, upper_panel, preferred_element_type...  23.4 us
    another operation x13, local copies, waits for them, and re-layouts  17.8 us
  transfers between devices with their start and end apart: 5, of which 5 were waited for; matrix products, arithmetic and copies ran while one was open for 22% of the time, Pallas kernels for 0%

commit v1 on v0

v1 whole, which is shorter than its diff:
```python
import functools

import jax
import jax.numpy as jnp
from jax import lax
from jax.experimental import pallas as pl
from jax.experimental.pallas import tpu as pltpu
from jax.sharding import PartitionSpec as P

F32 = jnp.float32
BF16 = jnp.bfloat16
VMEM_BYTES = 58 * 1024 * 1024
IN_VMEM = pl.BlockSpec(memory_space=pltpu.VMEM)
IN_SMEM = pl.BlockSpec(memory_space=pltpu.SMEM)


def dot(a, b):
    return jnp.dot(a, b, preferred_element_type=F32)


def params():
    return pltpu.CompilerParams(vmem_limit_bytes=VMEM_BYTES)


def head_kernel(panels, index, inverse, *refs):
    pieces, out = refs[:-1], refs[-1]
    for r, piece in enumerate(pieces):
        k = index[r]

        @pl.when(k < panels - 1)
        def _():
            out[k] = dot(inverse[k], piece[0]).astype(BF16)


def head(panels, index, inverse, pieces):
    tile = inverse.shape[1]
    return pl.pallas_call(
        functools.partial(head_kernel, panels),
        out_shape=jax.ShapeDtypeStruct((panels - 1, tile, tile), BF16),
        in_specs=[IN_SMEM] + [IN_VMEM] * (1 + len(pieces)),
        out_specs=IN_VMEM,
        compiler_params=params(),
    )(index, inverse, *pieces)


def lower_kernel(panels, parts, slot, row_first, inverse, *refs):
    columns, heads = refs[:parts], refs[parts : 2 * parts]
    out, raw, top, sem = refs[2 * parts :]
    rows, tile = raw.shape[1], raw.shape[3]
    per = panels // parts
    copies = []
    for i in range(parts):
        for j in range(per):
            k = slot[i * per + j]
            copies.append(pltpu.make_async_copy(columns[i].at[j], raw.at[k], sem.at[0, i * per + j]))
            copies.append(pltpu.make_async_copy(heads[i].at[j], top.at[k], sem.at[1, i * per + j]))
    for copy in copies:
        copy.start()
    for copy in copies:
        copy.wait()
    for k in range(panels):
        s = raw[k].reshape(rows * tile, tile)
        if k == 0:
            solved = dot(s, inverse[0])
        else:
            known = out[:, : k * tile]
            upper = top[k, :k].reshape(k * tile, tile)
            s = s.astype(F32) - dot(known, upper)
            high = s.astype(BF16)
            low = (s - high.astype(F32)).astype(BF16)
            solved = dot(high, inverse[k]) + dot(low, inverse[k])
        for a in range(rows):
            live = row_first[a] <= k
            block = solved[a * tile : (a + 1) * tile]
            out[a * tile : (a + 1) * tile, k * tile : (k + 1) * tile] = jnp.where(live, block, 0.0).astype(BF16)


def lower(panels, slot, row_first, inverse, columns, heads):
    parts = len(columns)
    rows, tile = columns[0].shape[1], columns[0].shape[2]
    any_space = pl.BlockSpec(memory_space=pl.ANY)
    return pl.pallas_call(
        functools.partial(lower_kernel, panels, parts),
        out_shape=jax.ShapeDtypeStruct((rows * tile, panels * tile), BF16),
        in_specs=[IN_SMEM, IN_SMEM, IN_VMEM] + [any_space] * (2 * parts),
        out_specs=IN_VMEM,
        scratch_shapes=[
            pltpu.VMEM((panels, rows, tile, tile), BF16),
            pltpu.VMEM((panels, panels - 1, tile, tile), BF16),
            pltpu.SemaphoreType.DMA((2, panels)),
        ],
        compiler_params=params(),
    )(slot, row_first, inverse, *columns, *heads)


def update_kernel(panels, skip, start, index, place, mask, inverse, lowers, *refs):
    pieces = refs[: len(refs) - 3 - (1 if start else 0)]
    matrix, out, upper = refs[len(pieces)], refs[-2], refs[-1]
    step = pl.program_id(0)
    c = step + start
    tile = inverse.shape[1]
    rows = lowers.shape[0] // tile
    row_at, column_at = place[0], place[1]
    for r, piece in enumerate(pieces):
        k = index[r]
        solved = dot(inverse[k], piece[step])
        live = mask[k, c] == 1
        upper[pl.ds(pl.multiple_of(k * tile, tile), tile), :] = jnp.where(live, solved, 0.0).astype(BF16)
    own = pl.ds(pl.multiple_of(jnp.minimum(row_at, panels - 1) * tile, tile), tile)
    for a in range(rows):
        s = matrix[a + skip, 0].astype(F32) - dot(lowers[a * tile : (a + 1) * tile, :], upper[...])
        out[a + skip, 0] = s.astype(BF16)
    if start == 0:

        @pl.when((step == 0) & (column_at < panels))
        def _():
            for k in range(panels):

                @pl.when(column_at == k)
                def _():
                    for a in range(rows):
                        out[a + skip, 0] = lowers[a * tile : (a + 1) * tile, k * tile : (k + 1) * tile]

    @pl.when(row_at < panels)
    def _():
        out[0, 0] = upper[own, :]


def update(panels, skip, start, index, place, mask, inverse, lowers, pieces, matrix, so_far):
    tile = inverse.shape[1]
    count = pieces[0].shape[0]
    column = pl.BlockSpec((matrix.shape[0], 1, tile, tile), lambda c: (0, c + start, 0, 0))
    operands = [index, place, mask, inverse, lowers, *pieces, matrix]
    specs = [IN_SMEM] * 3 + [IN_VMEM] * (2 + len(pieces)) + [column]
    aliases = {}
    if start:
        aliases = {len(operands): 0}
        operands.append(so_far)
        specs.append(pl.BlockSpec(memory_space=pl.ANY))
    flops = 2 * count * (lowers.shape[0] * lowers.shape[1] + panels * tile * tile) * tile
    return pl.pallas_call(
        functools.partial(update_kernel, panels, skip, start),
        out_shape=jax.ShapeDtypeStruct(matrix.shape, BF16),
        grid=(count,),
        in_specs=specs,
        out_specs=column,
        scratch_shapes=[pltpu.VMEM((panels * tile, tile), BF16)],
        input_output_aliases=aliases,
        cost_estimate=pl.CostEstimate(
            flops=flops, bytes_accessed=4 * count * matrix.shape[0] * tile * tile, transcendentals=0
        ),
        compiler_params=params(),
    )(*operands)


def rows_gathered(own):
    at = lax.axis_index("prow")
    before = lax.ppermute(own, "prow", [(0, 1), (1, 2), (2, 3), (3, 0)])
    after = lax.ppermute(own, "prow", [(1, 0), (2, 1), (3, 2), (0, 3)])
    passed = jnp.where(at == 2, before, jnp.where(at == 1, after, own))
    across = lax.ppermute(passed, "prow", [(0, 2), (3, 1), (2, 3), (1, 0)])
    return [own, before, after, across]


def to_far(block):
    return lax.ppermute(block, "pcol", [(0, 4), (1, 5), (2, 6), (3, 7)])


def beside_near(block):
    return lax.ppermute(block, "pcol", [(0, 2), (2, 0), (1, 3), (3, 1)])


def beside_far(block):
    return lax.ppermute(block, "pcol", [(4, 6), (6, 4), (5, 7), (7, 5)])


def diagonal(block):
    return lax.ppermute(block, "pcol", [(0, 6), (1, 7), (2, 4), (3, 5)])


def twin(block):
    return lax.ppermute(block, "pcol", [(i, i ^ 1) for i in range(8)])


def local(small, matrix, lower_inverse, upper_inverse, row_first, col_mask):
    panels, tile = lower_inverse.shape[0], lower_inverse.shape[1]
    local_rows, local_cols = matrix.shape[0], matrix.shape[2]
    grid = matrix.reshape(local_rows, local_cols, tile, tile)
    mask = col_mask.reshape(panels, local_cols)
    row_at, column_at = lax.axis_index("prow"), lax.axis_index("pcol")
    place = jnp.stack([row_at, column_at]).astype(jnp.int32)
    skip = 1 if small else 0
    first = row_first.reshape(local_rows)[skip:]
    if small:
        cut = 2
        near = column_at < 4
        index = jnp.mod(row_at + jnp.array([0, 3, 1, 2]), 4).astype(jnp.int32)
        chunks = [rows_gathered(grid[0, :cut]), rows_gathered(grid[0, cut:])]
        half = (local_rows - 1 + 1) // 2
        col_a, col_b = grid[1 : 1 + half, 0], grid[1 + half :, 0]
        far_a, far_b = to_far(col_a), to_far(col_b)
        side_a, side_b = beside_near(col_a), beside_near(col_b)
        cross_a, cross_b = beside_far(far_a), beside_far(far_b)
        mine = jnp.stack(
            [
                jnp.where(near, jnp.concatenate([col_a, col_b]), jnp.concatenate([far_a, far_b])),
                jnp.where(near, jnp.concatenate([side_a, side_b]), jnp.concatenate([cross_a, cross_b])),
            ]
        )
        other = twin(mine)
        tops = head(panels, index, lower_inverse, chunks[0])
        heads = jnp.stack(
            [
                jnp.where(near, tops, to_far(tops)),
                jnp.where(near, beside_near(tops), diagonal(tops)),
            ]
        )
        other_heads = twin(heads)
        slot = jnp.bitwise_xor(jnp.bitwise_and(column_at, 3), jnp.array([0, 2, 1, 3])).astype(jnp.int32)
        lowers = lower(panels, slot, first, upper_inverse, [mine, other], [heads, other_heads])
    else:
        natural = jnp.arange(panels, dtype=jnp.int32)
        index = natural
        rows = lax.all_gather(grid[0], "prow")[:panels]
        chunks = [[rows[k] for k in range(panels)]]
        columns = jnp.where(natural[:, None, None, None] == column_at, grid[None, :, 0], 0)
        columns = lax.psum(columns, "pcol")
        tops = head(panels, index, lower_inverse, chunks[0])
        heads = jnp.where(natural[:, None, None, None] == column_at, tops[None], 0)
        heads = lax.psum(heads, "pcol")
        lowers = lower(panels, natural, first, upper_inverse, [columns], [heads])
    result, start = None, 0
    for pieces in chunks:
        result = update(
            panels, skip, start, index, place, mask, lower_inverse, lowers, pieces, grid, result
        )
        start += pieces[0].shape[0]
    return result.reshape(matrix.shape)


def solution(mesh):
    small = mesh.shape["prow"] == 4 and mesh.shape["pcol"] == 8

    def step(matrix, lower_inverse, upper_inverse, row_first, col_mask):
        fits = small and lower_inverse.shape[0] == 4 and matrix.shape[0] > 2 and matrix.shape[2] > 2
        return jax.shard_map(
            functools.partial(local, fits),
            mesh=mesh,
            in_specs=(
                P(None, "prow", None, "pcol", None, None),
                P(),
                P(),
                P(None, "prow"),
                P(None, None, "pcol"),
            ),
            out_specs=P(None, "prow", None, "pcol", None, None),
            check_vma=False,
        )(matrix, lower_inverse, upper_inverse, row_first, col_mask)

    return step
```

time: 527 us -> 104 us (0.20); the launches traced: 518 us -> 103 us
  local copies, waits for them, and re-layouts: 210 us -> 7.9 us
  waiting for transfers between devices: 206 us -> 18.4 us
  loops' own time: 40.6 us -> 0 us
  starting transfers between devices: 0.35 us -> 39.6 us
  Pallas kernels: 0 us -> 28.3 us
  matrix products: 27.5 us -> 0 us
  between operations: 13.4 us -> 0.3 us
  other arithmetic: 19.9 us -> 8.93 us
    psum x5 -> x0, waiting for transfers between devices: 206 us -> none  [spread(): return lax.psum(block, axis)]
    squeeze x64 -> x2, local copies, waits for them, and re-layouts: 72.9 us -> 1.99 us  [local(): chunks = [rows_gathered(grid[0, :cut]), rows_gathered(grid[0, cut:])]]
    dynamic_update_slice x64 -> x0, local copies, waits for them, and re-layouts: 50.2 us -> none  [apply_update(): return lax.map(update_row, (block, lower_panel, row_live))]
    another operation x80 -> x0, loops' own time: 40.6 us -> none  [the longest x8 39.9 us: apply_update(): return lax.map(update_row, (block, lower_panel, row_live))]
    dynamic_slice x64 -> x0, local copies, waits for them, and re-layouts: 39.8 us -> none  [apply_update(): return lax.map(update_row, (block, lower_panel, row_live))]
    ppermute x0 -> x17, starting transfers between devices: none -> 39.6 us  [the longest x3 11.7 us: to_far(): return lax.ppermute(block, 'pcol', [(0, 4), (1, 5), (2, 6), (3, 7)])]
    pallas_call x0 -> x4, Pallas kernels: none -> 28.3 us  [the longest x2 16.4 us: update(): pl.pallas_call(functools.partial(update_kernel, panels, skip, start), out...]
    dot_general x22 -> x0, matrix products: 27.5 us -> none  [the longest x20 23.4 us: update_row(): jnp.einsum('ab,jbc->jac', lower_tile, upper_panel, preferred_element_type...]
  transfers between devices with their start and end apart: 5 -> 17, of which waited for: 5 -> 5; matrix products, arithmetic and copies ran while one was open for 22% -> 13% of each run, Pallas kernels for 0% -> 19%
where the time goes in v1:
time: 104 us; the launch traced here: 103 us
  starting transfers between devices  39.6 us (38%)
  Pallas kernels  28.3 us (27%)
  waiting for transfers between devices  18.4 us (18%)
  other arithmetic  8.93 us (9%)
  local copies, waits for them, and re-layouts  7.9 us (8%)
    pallas_call x2, Pallas kernels, update(): pl.pallas_call(functools.partial(update_kernel, panels, skip, start), out...  16.4 us
    ppermute x3, starting transfers between devices, to_far(): return lax.ppermute(block, 'pcol', [(0, 4), (1, 5), (2, 6), (3, 7)])  11.7 us
    pallas_call x1, Pallas kernels, lower(): pl.pallas_call(functools.partial(lower_kernel, panels, parts), out_shape=...  9.24 us
    ppermute x3, starting transfers between devices, beside_near(): return lax.ppermute(block, 'pcol', [(0, 2), (2, 0), (1, 3), (3, 1)])  9.21 us
    ppermute x3, waiting for transfers between devices, beside_near(): return lax.ppermute(block, 'pcol', [(0, 2), (2, 0), (1, 3), (3, 1)])  9.11 us
    ppermute x2, waiting for transfers between devices, rows_gathered(): before = lax.ppermute(own, 'prow', [(0, 1), (1, 2), (2, 3), (3, 0)])  7.63 us
    ppermute x2, starting transfers between devices, rows_gathered(): after = lax.ppermute(own, 'prow', [(1, 0), (2, 1), (3, 2), (0, 3)])  7.31 us
    ppermute x1, starting transfers between devices, diagonal(): return lax.ppermute(block, 'pcol', [(0, 6), (1, 7), (2, 4), (3, 5)])  6.76 us
  transfers between devices with their start and end apart: 17, of which 5 were waited for; matrix products, arithmetic and copies ran while one was open for 13% of the time, Pallas kernels for 19%

profile of v1, /device:TPU:0, one launch (start us, length us, event | category | flops | bytes accessed | tf_op | source)
XLA Modules:
  0.0 103.4 jit_solution(11568550066221926996)
XLA Ops:
  0.0 1.1 %slice_bitcast_fusion.1 = (bf16[1,4,256,256]{3,2,1,0:T(8,128)(2,1)S(1)}, bf16[4,256,256]{2,1,0:T(8,128)(2,1)S(1)}) fusion(bf16[8,5,256,256]{3,2,1,0:T(8,128)(2,1)} %bitcast.35), kind=kLoop, calls=%fused_computation.5 | loop fusion | bytes 1572864 | tf_op jit(solution)/shard_map/concatenate | solution.py:206
  1.1 5.7 %collective-permute-start = (bf16[4,256,256]{2,1,0:T(8,128)(2,1)S(1)}, bf16[4,256,256]{2,1,0:T(8,128)(2,1)}, u32[]{:S(2)}, u32[]{:S(2)}) collective-permute-start(bf16[4,256,256]{2,1,0:T(8,128)(2,1)S(1)} %get-tuple-element.6), channel_id=1, source_target_pairs={{0,4},{1,5},{2,6},{3,7},{8,12},{9,13},{10,14},{11,15},{16,20},{17,... | collective-permute-start | bytes 1572872 | tf_op jit(solution)/shard_map/ppermute | solution.py:166
  6.8 1.0 slice_bitcast_fusion.5.refs_0_
  7.8 3.7 %collective-permute-start.8 = (bf16[2,256,256]{2,1,0:T(8,128)(2,1)S(1)}, bf16[2,256,256]{2,1,0:T(8,128)(2,1)S(1)}, u32[]{:S(2)}, u32[]{:S(2)}) collective-permute-start(bf16[2,256,256]{2,1,0:T(8,128)(2,1)S(1)} %slice_bitcast_fusion.5.refs_0_), channel_id=1, source_target_pairs={{8,0},{16,8},{24,16},{0,24},{9,1},{17,9},{25,17},{1,25},{10,2},{18... | collective-permute-start | bytes 786440 | tf_op jit(solution)/shard_map/ppermute | solution.py:159
  11.4 1.8 %slice_bitcast_fusion.4 = (bf16[1,3,256,256]{3,2,1,0:T(8,128)(2,1)S(1)}, bf16[3,256,256]{2,1,0:T(8,128)(2,1)}) fusion(bf16[8,5,256,256]{3,2,1,0:T(8,128)(2,1)} %bitcast.37), kind=kLoop, calls=%fused_computation.11 | loop fusion | bytes 1179648 | tf_op jit(solution)/shard_map/concatenate | solution.py:206
  13.2 2.0 %collective-permute-start.1 = (bf16[3,256,256]{2,1,0:T(8,128)(2,1)}, bf16[3,256,256]{2,1,0:T(8,128)(2,1)}, u32[]{:S(2)}, u32[]{:S(2)}) collective-permute-start(bf16[3,256,256]{2,1,0:T(8,128)(2,1)} %get-tuple-element.8), channel_id=1, source_target_pairs={{0,4},{1,5},{2,6},{3,7},{8,12},{9,13},{10,14},{11,15},{16,20},{17,... | collective-permute-start | bytes 1179656 | tf_op jit(solution)/shard_map/ppermute | solution.py:166
  15.3 3.4 %collective-permute-start.2 = (bf16[4,256,256]{2,1,0:T(8,128)(2,1)S(1)}, bf16[4,256,256]{2,1,0:T(8,128)(2,1)}, u32[]{:S(2)}, u32[]{:S(2)}) collective-permute-start(bf16[4,256,256]{2,1,0:T(8,128)(2,1)S(1)} %get-tuple-element.6), channel_id=1, source_target_pairs={{0,2},{2,0},{1,3},{3,1},{8,10},{10,8},{9,11},{11,9},{16,18},{18,16... | collective-permute-start | bytes 1572872 | tf_op jit(solution)/shard_map/ppermute | solution.py:170
  18.7 1.5 %collective-permute-start.4 = (bf16[4,256,256]{2,1,0:T(8,128)(2,1)}, bf16[4,256,256]{2,1,0:T(8,128)(2,1)}, u32[]{:S(2)}, u32[]{:S(2)}) collective-permute-start(bf16[4,256,256]{2,1,0:T(8,128)(2,1)} %collective-permute-done), channel_id=1, source_target_pairs={{4,6},{6,4},{5,7},{7,5},{12,14},{14,12},{13,15},{15,13},{20,22},{2... | collective-permute-start | bytes 1572872 | tf_op jit(solution)/shard_map/ppermute | solution.py:174
  20.2 3.1 %collective-permute-done.7.refs_1_ = bf16[2,256,256]{2,1,0:T(8,128)(2,1)S(1)} collective-permute-done((bf16[2,256,256]{2,1,0:T(8,128)(2,1)S(1)}, bf16[2,256,256]{2,1,0:T(8,128)(2,1)S(1)}, u32[]{:S(2)}, u32[]{:S(2)}) %collective-permute-start.7) | collective-permute-done | bytes 262176 | tf_op jit(solution)/shard_map/ppermute | solution.py:158
  23.2 1.1 %select_select_fusion.1 = bf16[2,256,256]{2,1,0:T(8,128)(2,1)S(1)} fusion(bf16[2,256,256]{2,1,0:T(8,128)(2,1)S(1)} %collective-permute-done.7.refs_1_, bf16[2,256,256]{2,1,0:T(8,128)(2,1)S(1)} %collective-permute-done.8.refs_2_, pred[]{:T(512)S(6)} %eq.11, pred[]{:T(512)S(6)} %eq.10, bf16[8,5,256,256]{3,2,1,0:T(8,128)(2,1)} %bitcast.38), kind=kLoop, calls=%fused_computation.13 | loop fusion | flops 262144 | bytes 1048578 | tf_op jit(solution)/shard_map/jit(_where)/select_n | solution.py:160
  24.3 0.8 collective-permute-start.9
  25.1 3.4 %collective-permute-start.3 = (bf16[3,256,256]{2,1,0:T(8,128)(2,1)}, bf16[3,256,256]{2,1,0:T(8,128)(2,1)}, u32[]{:S(2)}, u32[]{:S(2)}) collective-permute-start(bf16[3,256,256]{2,1,0:T(8,128)(2,1)} %get-tuple-element.8), channel_id=1, source_target_pairs={{0,2},{2,0},{1,3},{3,1},{8,10},{10,8},{9,11},{11,9},{16,18},{18,16... | collective-permute-start | bytes 1179656 | tf_op jit(solution)/shard_map/ppermute | solution.py:170
  28.5 1.4 %collective-permute-start.5 = (bf16[3,256,256]{2,1,0:T(8,128)(2,1)}, bf16[3,256,256]{2,1,0:T(8,128)(2,1)}, u32[]{:S(2)}, u32[]{:S(2)}) collective-permute-start(bf16[3,256,256]{2,1,0:T(8,128)(2,1)} %collective-permute-done.1), channel_id=1, source_target_pairs={{4,6},{6,4},{5,7},{7,5},{12,14},{14,12},{13,15},{15,13},{20,22},{2... | collective-permute-start | bytes 1179656 | tf_op jit(solution)/shard_map/ppermute | solution.py:174
  29.9 1.2 %and_select_fusion.index = s32[4]{0:T(128)} fusion(s32[4]{0:T(128)} %constant.32.clone, s32[]{:T(128)} %axis_index.15), kind=kLoop, calls=%fused_computation.16 | loop fusion | flops 48 | bytes 36 | tf_op jit(solution)/shard_map/jit(remainder)/select_n | solution.py:197
  32.0 2.7 %shard_map.73 = bf16[3,256,256]{2,1,0:T(8,128)(2,1)} custom-call(s32[4]{0:T(128)} %and_select_fusion.index, bf16[4,256,256]{2,1,0:T(8,128)(2,1)} %inverse.7, bf16[2,256,256]{2,1,0:T(8,128)(2,1)} %copy-done.4, bf16[2,256,256]{2,1,0:T(8,128)(2,1)} %copy-done.3, bf16[2,256,256]{2,1,0:T(8,128)(2,1)} %copy-done.2, bf16[2,256,256]{2,1,0:T(8,128)(2,1)} %copy-done.9), custom_call_target="tpu_custom_call" | custom-call | tf_op jit(solution)/shard_map/pallas_call | solution.py:37
  34.7 4.0 %collective-permute-start.10 = (bf16[3,256,256]{2,1,0:T(8,128)(2,1)}, bf16[3,256,256]{2,1,0:T(8,128)(2,1)S(1)}, u32[]{:S(2)}, u32[]{:S(2)}) collective-permute-start(bf16[3,256,256]{2,1,0:T(8,128)(2,1)} %shard_map.73), channel_id=1, source_target_pairs={{0,4},{1,5},{2,6},{3,7},{8,12},{9,13},{10,14},{11,15},{16,20},{17,... | collective-permute-start | bytes 1179656 | tf_op jit(solution)/shard_map/ppermute | solution.py:166
  38.7 1.3 %maximum_select_fusion = bf16[1,7,256,256]{3,2,1,0:T(8,128)(2,1)S(1)} fusion(bf16[1,3,256,256]{3,2,1,0:T(8,128)(2,1)S(1)} %get-tuple-element.7, bf16[1,4,256,256]{3,2,1,0:T(8,128)(2,1)S(1)} %get-tuple-element.5, bf16[1,3,256,256]{3,2,1,0:T(8,128)(2,1)} %bitcast.10, bf16[1,4,256,256]{3,2,1,0:T(8,128)(2,1)} %bitcast.8, pred[]{:T(512)S(6)} %lt.10), kind=kLoop, calls=%fused_computation.1 | loop fusion | flops 1376256 | bytes 2752513 | tf_op jit(solution)/shard_map/jit(_where)/select_n | solution.py:206
  40.0 1.6 %maximum_select_fusion.1 = bf16[1,7,256,256]{3,2,1,0:T(8,128)(2,1)S(1)} fusion(bf16[1,3,256,256]{3,2,1,0:T(8,128)(2,1)} %bitcast.12, bf16[1,4,256,256]{3,2,1,0:T(8,128)(2,1)} %bitcast.11, bf16[1,3,256,256]{3,2,1,0:T(8,128)(2,1)} %bitcast.14, bf16[1,4,256,256]{3,2,1,0:T(8,128)(2,1)} %bitcast.13, pred[]{:T(512)S(6)} %lt.10), kind=kLoop, calls=%fused_computation.2 | loop fusion | flops 1376256 | bytes 2752513 | tf_op jit(solution)/shard_map/jit(_where)/select_n | solution.py:207
  41.9 6.8 %collective-permute-start.12 = (bf16[3,256,256]{2,1,0:T(8,128)(2,1)S(1)}, bf16[3,256,256]{2,1,0:T(8,128)(2,1)}, u32[]{:S(2)}, u32[]{:S(2)}) collective-permute-start(bf16[3,256,256]{2,1,0:T(8,128)(2,1)S(1)} %copy-done.5), channel_id=1, source_target_pairs={{0,6},{1,7},{2,4},{3,5},{8,14},{9,15},{10,12},{11,13},{16,22},{17,... | collective-permute-start | bytes 1179656 | tf_op jit(solution)/shard_map/ppermute | solution.py:178
  48.7 2.4 %collective-permute-start.11 = (bf16[3,256,256]{2,1,0:T(8,128)(2,1)S(1)}, bf16[3,256,256]{2,1,0:T(8,128)(2,1)}, u32[]{:S(2)}, u32[]{:S(2)}) collective-permute-start(bf16[3,256,256]{2,1,0:T(8,128)(2,1)S(1)} %copy-done.5), channel_id=1, source_target_pairs={{0,2},{2,0},{1,3},{3,1},{8,10},{10,8},{9,11},{11,9},{16,18},{18,16... | collective-permute-start | bytes 1179656 | tf_op jit(solution)/shard_map/ppermute | solution.py:170
  51.1 1.0 slice_bitcast_fusion.2.refs_0_
  52.1 3.7 %collective-permute-start.15 = (bf16[3,256,256]{2,1,0:T(8,128)(2,1)S(1)}, bf16[3,256,256]{2,1,0:T(8,128)(2,1)S(1)}, u32[]{:S(2)}, u32[]{:S(2)}) collective-permute-start(bf16[3,256,256]{2,1,0:T(8,128)(2,1)S(1)} %slice_bitcast_fusion.2.refs_0_), channel_id=1, source_target_pairs={{8,0},{16,8},{24,16},{0,24},{9,1},{17,9},{25,17},{1,25},{10,2},{18... | collective-permute-start | bytes 1179656 | tf_op jit(solution)/shard_map/ppermute | solution.py:159
  55.9 1.5 %collective-permute-done.12 = bf16[3,256,256]{2,1,0:T(8,128)(2,1)} collective-permute-done((bf16[3,256,256]{2,1,0:T(8,128)(2,1)S(1)}, bf16[3,256,256]{2,1,0:T(8,128)(2,1)}, u32[]{:S(2)}, u32[]{:S(2)}) %collective-permute-start.12) | collective-permute-done | bytes 393248 | tf_op jit(solution)/shard_map/ppermute | solution.py:178
  57.3 9.1 %collective-permute-done.11 = bf16[3,256,256]{2,1,0:T(8,128)(2,1)} collective-permute-done((bf16[3,256,256]{2,1,0:T(8,128)(2,1)S(1)}, bf16[3,256,256]{2,1,0:T(8,128)(2,1)}, u32[]{:S(2)}, u32[]{:S(2)}) %collective-permute-start.11) | collective-permute-done | bytes 393248 | tf_op jit(solution)/shard_map/ppermute | solution.py:170
  66.4 1.0 %select_bitcast_fusion = bf16[1,3,256,256]{3,2,1,0:T(8,128)(2,1)S(1)} fusion(bf16[3,256,256]{2,1,0:T(8,128)(2,1)} %collective-permute-done.11, bf16[3,256,256]{2,1,0:T(8,128)(2,1)} %collective-permute-done.12, pred[]{:T(512)S(6)} %lt.10), kind=kLoop, calls=%fused_computation.8 | loop fusion | flops 196608 | bytes 1179649 | tf_op jit(solution)/shard_map/stack | solution.py:212
  69.0 4.6 %collective-permute-done.14.refs_1_ = bf16[3,256,256]{2,1,0:T(8,128)(2,1)S(1)} collective-permute-done((bf16[3,256,256]{2,1,0:T(8,128)(2,1)S(1)}, bf16[3,256,256]{2,1,0:T(8,128)(2,1)S(1)}, u32[]{:S(2)}, u32[]{:S(2)}) %collective-permute-start.14) | collective-permute-done | bytes 393248 | tf_op jit(solution)/shard_map/ppermute | solution.py:158
  73.6 1.2 %select_select_fusion = bf16[3,256,256]{2,1,0:T(8,128)(2,1)S(1)} fusion(bf16[3,256,256]{2,1,0:T(8,128)(2,1)S(1)} %collective-permute-done.14.refs_1_, bf16[3,256,256]{2,1,0:T(8,128)(2,1)S(1)} %collective-permute-done.15.refs_2_, pred[]{:T(512)S(6)} %eq.11, pred[]{:T(512)S(6)} %eq.10, bf16[8,5,256,256]{3,2,1,0:T(8,128)(2,1)} %bitcast.40), kind=kLoop, calls=%fused_computation.7 | loop fusion | flops 393216 | bytes 1572866 | tf_op jit(solution)/shard_map/jit(_where)/select_n | solution.py:160
  74.8 0.8 collective-permute-start.16
  76.1 0.9 copy-done.10
  77.0 9.2 %shard_map.74.lowers = bf16[1792,1024]{1,0:T(8,128)(2,1)} custom-call(s32[4]{0:T(128)} %broadcast_xor_fusion.slot, s32[7]{0:T(128)} %slice_bitcast_fusion.6.row_first, bf16[4,256,256]{2,1,0:T(8,128)(2,1)} %inverse.5, bf16[2,7,256,256]{3,2,1,0:T(8,128)(2,1)} %copy-done, bf16[2,7,256,256]{3,2,1,0:T(8,128)(2,1)} %collective-permute-done.6.refs_1_, ...), custom_call_target="tpu_custom_call" | custom-call | tf_op jit(solution)/shard_map/pallas_call | solution.py:82
  86.3 7.3 %shard_map.75.refs_5_ = bf16[8,5,256,256]{3,2,1,0:T(8,128)(2,1)} custom-call(s32[4]{0:T(128)} %and_select_fusion.index, s32[2]{0:T(128)} %pad_add_fusion.place, s32[4,5]{1,0:T(4,128)} %bitcast.43, bf16[4,256,256]{2,1,0:T(8,128)(2,1)} %inverse.7, bf16[1792,1024]{1,0:T(8,128)(2,1)} %shard_map.74.lowers, bf16[2,256,256]{2,1,0:T(8,128)(2,1)} %copy-done.4, ...), custom_call_target="tpu_custom_call" | custom-call | flops 2147483648 | bytes 4194304 | tf_op jit(solution)/shard_map/pallas_call | solution.py:141
  94.3 9.0 %shard_map.76 = bf16[8,5,256,256]{3,2,1,0:T(8,128)(2,1)} custom-call(s32[4]{0:T(128)} %and_select_fusion.index, s32[2]{0:T(128)} %pad_add_fusion.place, s32[4,5]{1,0:T(4,128)} %bitcast.44, bf16[4,256,256]{2,1,0:T(8,128)(2,1)} %inverse.7, bf16[1792,1024]{1,0:T(8,128)(2,1)} %shard_map.74.lowers, ...), custom_call_target="tpu_custom_call", output_to_operand_aliasing={{}: (10, {})} | custom-call | flops 3221225472 | bytes 6291456 | tf_op jit(solution)/shard_map/pallas_call | solution.py:141
  (50 shorter events, 4.0 us)
Async XLA Ops:
  1.1 17.6 %collective-permute-start = (bf16[4,256,256]{2,1,0:T(8,128)(2,1)S(1)}, bf16[4,256,256]{2,1,0:T(8,128)(2,1)}, u32[]{:S(2)}, u32[]{:S(2)}) collective-permute-start(bf16[4,256,256]{2,1,0:T(8,128)(2,1)S(1)} %get-tuple-element.6), channel_id=1, source_target_pairs={{0,4},{1,5},{2,6},{3,7},{8,12},{9,13},{10,14},{11,15},{16,20},{17,... | collective-permute-start | bytes 1572872 | tf_op jit(solution)/shard_map/ppermute | solution.py:166
  7.8 23.5 %copy-start.4 = (bf16[2,256,256]{2,1,0:T(8,128)(2,1)}, bf16[2,256,256]{2,1,0:T(8,128)(2,1)S(1)}, u32[]{:S(2)}) copy-start(bf16[2,256,256]{2,1,0:T(8,128)(2,1)S(1)} %slice_bitcast_fusion.5.refs_0_) | copy-start | bytes 786436
  7.8 12.4 %collective-permute-start.8 = (bf16[2,256,256]{2,1,0:T(8,128)(2,1)S(1)}, bf16[2,256,256]{2,1,0:T(8,128)(2,1)S(1)}, u32[]{:S(2)}, u32[]{:S(2)}) collective-permute-start(bf16[2,256,256]{2,1,0:T(8,128)(2,1)S(1)} %slice_bitcast_fusion.5.refs_0_), channel_id=1, source_target_pairs={{8,0},{16,8},{24,16},{0,24},{9,1},{17,9},{25,17},{1,25},{10,2},{18... | collective-permute-start | bytes 786440 | tf_op jit(solution)/shard_map/ppermute | solution.py:159
  11.4 11.8 %collective-permute-start.7 = (bf16[2,256,256]{2,1,0:T(8,128)(2,1)S(1)}, bf16[2,256,256]{2,1,0:T(8,128)(2,1)S(1)}, u32[]{:S(2)}, u32[]{:S(2)}) collective-permute-start(bf16[2,256,256]{2,1,0:T(8,128)(2,1)S(1)} %slice_bitcast_fusion.5.refs_0_), channel_id=1, source_target_pairs={{0,8},{8,16},{16,24},{24,0},{1,9},{9,17},{17,25},{25,1},{2,10},{10... | collective-permute-start | bytes 786440 | tf_op jit(solution)/shard_map/ppermute | solution.py:158
  13.2 15.3 %collective-permute-start.1 = (bf16[3,256,256]{2,1,0:T(8,128)(2,1)}, bf16[3,256,256]{2,1,0:T(8,128)(2,1)}, u32[]{:S(2)}, u32[]{:S(2)}) collective-permute-start(bf16[3,256,256]{2,1,0:T(8,128)(2,1)} %get-tuple-element.8), channel_id=1, source_target_pairs={{0,4},{1,5},{2,6},{3,7},{8,12},{9,13},{10,14},{11,15},{16,20},{17,... | collective-permute-start | bytes 1179656 | tf_op jit(solution)/shard_map/ppermute | solution.py:166
  15.3 24.7 %collective-permute-start.2 = (bf16[4,256,256]{2,1,0:T(8,128)(2,1)S(1)}, bf16[4,256,256]{2,1,0:T(8,128)(2,1)}, u32[]{:S(2)}, u32[]{:S(2)}) collective-permute-start(bf16[4,256,256]{2,1,0:T(8,128)(2,1)S(1)} %get-tuple-element.6), channel_id=1, source_target_pairs={{0,2},{2,0},{1,3},{3,1},{8,10},{10,8},{9,11},{11,9},{16,18},{18,16... | collective-permute-start | bytes 1572872 | tf_op jit(solution)/shard_map/ppermute | solution.py:170
  18.7 21.3 %collective-permute-start.4 = (bf16[4,256,256]{2,1,0:T(8,128)(2,1)}, bf16[4,256,256]{2,1,0:T(8,128)(2,1)}, u32[]{:S(2)}, u32[]{:S(2)}) collective-permute-start(bf16[4,256,256]{2,1,0:T(8,128)(2,1)} %collective-permute-done), channel_id=1, source_target_pairs={{4,6},{6,4},{5,7},{7,5},{12,14},{14,12},{13,15},{15,13},{20,22},{2... | collective-permute-start | bytes 1572872 | tf_op jit(solution)/shard_map/ppermute | solution.py:174
  20.2 11.1 %copy-start.2 = (bf16[2,256,256]{2,1,0:T(8,128)(2,1)}, bf16[2,256,256]{2,1,0:T(8,128)(2,1)S(1)}, u32[]{:S(2)}) copy-start(bf16[2,256,256]{2,1,0:T(8,128)(2,1)S(1)} %collective-permute-done.8.refs_2_) | copy-start | bytes 786436
  23.2 8.0 %copy-start.3 = (bf16[2,256,256]{2,1,0:T(8,128)(2,1)}, bf16[2,256,256]{2,1,0:T(8,128)(2,1)S(1)}, u32[]{:S(2)}) copy-start(bf16[2,256,256]{2,1,0:T(8,128)(2,1)S(1)} %collective-permute-done.7.refs_1_) | copy-start | bytes 786436
  24.3 6.9 %collective-permute-start.9 = (bf16[2,256,256]{2,1,0:T(8,128)(2,1)S(1)}, bf16[2,256,256]{2,1,0:T(8,128)(2,1)S(1)}, u32[]{:S(2)}, u32[]{:S(2)}) collective-permute-start(bf16[2,256,256]{2,1,0:T(8,128)(2,1)S(1)} %select_select_fusion.1), channel_id=1, source_target_pairs={{0,16},{24,8},{16,24},{8,0},{1,17},{25,9},{17,25},{9,1},{2,18},{26... | collective-permute-start | bytes 786440 | tf_op jit(solution)/shard_map/ppermute | solution.py:161
  25.1 14.8 %collective-permute-start.3 = (bf16[3,256,256]{2,1,0:T(8,128)(2,1)}, bf16[3,256,256]{2,1,0:T(8,128)(2,1)}, u32[]{:S(2)}, u32[]{:S(2)}) collective-permute-start(bf16[3,256,256]{2,1,0:T(8,128)(2,1)} %get-tuple-element.8), channel_id=1, source_target_pairs={{0,2},{2,0},{1,3},{3,1},{8,10},{10,8},{9,11},{11,9},{16,18},{18,16... | collective-permute-start | bytes 1179656 | tf_op jit(solution)/shard_map/ppermute | solution.py:170
  28.5 11.5 %collective-permute-start.5 = (bf16[3,256,256]{2,1,0:T(8,128)(2,1)}, bf16[3,256,256]{2,1,0:T(8,128)(2,1)}, u32[]{:S(2)}, u32[]{:S(2)}) collective-permute-start(bf16[3,256,256]{2,1,0:T(8,128)(2,1)} %collective-permute-done.1), channel_id=1, source_target_pairs={{4,6},{6,4},{5,7},{7,5},{12,14},{14,12},{13,15},{15,13},{20,22},{2... | collective-permute-start | bytes 1179656 | tf_op jit(solution)/shard_map/ppermute | solution.py:174
  31.3 0.7 copy-start.9
  34.7 7.2 %copy-start.5 = (bf16[3,256,256]{2,1,0:T(8,128)(2,1)S(1)}, bf16[3,256,256]{2,1,0:T(8,128)(2,1)}, u32[]{:S(2)}) copy-start(bf16[3,256,256]{2,1,0:T(8,128)(2,1)} %shard_map.73) | copy-start | bytes 1179652
  34.7 21.1 %collective-permute-start.10 = (bf16[3,256,256]{2,1,0:T(8,128)(2,1)}, bf16[3,256,256]{2,1,0:T(8,128)(2,1)S(1)}, u32[]{:S(2)}, u32[]{:S(2)}) collective-permute-start(bf16[3,256,256]{2,1,0:T(8,128)(2,1)} %shard_map.73), channel_id=1, source_target_pairs={{0,4},{1,5},{2,6},{3,7},{8,12},{9,13},{10,14},{11,15},{16,20},{17,... | collective-permute-start | bytes 1179656 | tf_op jit(solution)/shard_map/ppermute | solution.py:166
  40.0 28.3 %copy-start.12 = (s32[8,1]{0,1:T(1,128)S(1)}, s32[8,1]{0,1:T(1,128)}, u32[]{:S(2)}) copy-start(s32[8,1]{0,1:T(1,128)} %param.10) | copy-start | bytes 100
  41.6 34.0 %copy-start.13 = (s32[4]{0:T(128)S(1)}, s32[4]{0:T(128)}, u32[]{:S(2)}) copy-start(s32[4]{0:T(128)} %constant.33.clone) | copy-start | bytes 52
  41.8 34.3 %copy-start = (bf16[2,7,256,256]{3,2,1,0:T(8,128)(2,1)}, bf16[2,7,256,256]{3,2,1,0:T(8,128)(2,1)S(1)}, u32[]{:S(2)}) copy-start(bf16[2,7,256,256]{3,2,1,0:T(8,128)(2,1)S(1)} %pad_maximum_fusion.refs_0_) | copy-start | bytes 5505028
  41.8 34.3 %collective-permute-start.6 = (bf16[2,7,256,256]{3,2,1,0:T(8,128)(2,1)S(1)}, bf16[2,7,256,256]{3,2,1,0:T(8,128)(2,1)}, u32[]{:S(2)}, u32[]{:S(2)}) collective-permute-start(bf16[2,7,256,256]{3,2,1,0:T(8,128)(2,1)S(1)} %pad_maximum_fusion.refs_0_), channel_id=1, source_target_pairs={{0,1},{1,0},{2,3},{3,2},{4,5},{5,4},{6,7},{7,6},{8,9},{9,8},{10,11... | collective-permute-start | bytes 5505032 | tf_op jit(solution)/shard_map/ppermute | solution.py:182
  41.9 15.4 %collective-permute-start.12 = (bf16[3,256,256]{2,1,0:T(8,128)(2,1)S(1)}, bf16[3,256,256]{2,1,0:T(8,128)(2,1)}, u32[]{:S(2)}, u32[]{:S(2)}) collective-permute-start(bf16[3,256,256]{2,1,0:T(8,128)(2,1)S(1)} %copy-done.5), channel_id=1, source_target_pairs={{0,6},{1,7},{2,4},{3,5},{8,14},{9,15},{10,12},{11,13},{16,22},{17,... | collective-permute-start | bytes 1179656 | tf_op jit(solution)/shard_map/ppermute | solution.py:178
  48.7 17.8 %collective-permute-start.11 = (bf16[3,256,256]{2,1,0:T(8,128)(2,1)S(1)}, bf16[3,256,256]{2,1,0:T(8,128)(2,1)}, u32[]{:S(2)}, u32[]{:S(2)}) collective-permute-start(bf16[3,256,256]{2,1,0:T(8,128)(2,1)S(1)} %copy-done.5), channel_id=1, source_target_pairs={{0,2},{2,0},{1,3},{3,1},{8,10},{10,8},{9,11},{11,9},{16,18},{18,16... | collective-permute-start | bytes 1179656 | tf_op jit(solution)/shard_map/ppermute | solution.py:170
  52.1 34.1 %copy-start.6 = (bf16[3,256,256]{2,1,0:T(8,128)(2,1)}, bf16[3,256,256]{2,1,0:T(8,128)(2,1)S(1)}, u32[]{:S(2)}) copy-start(bf16[3,256,256]{2,1,0:T(8,128)(2,1)S(1)} %slice_bitcast_fusion.2.refs_0_) | copy-start | bytes 1179652
  52.1 16.9 %collective-permute-start.15 = (bf16[3,256,256]{2,1,0:T(8,128)(2,1)S(1)}, bf16[3,256,256]{2,1,0:T(8,128)(2,1)S(1)}, u32[]{:S(2)}, u32[]{:S(2)}) collective-permute-start(bf16[3,256,256]{2,1,0:T(8,128)(2,1)S(1)} %slice_bitcast_fusion.2.refs_0_), channel_id=1, source_target_pairs={{8,0},{16,8},{24,16},{0,24},{9,1},{17,9},{25,17},{1,25},{10,2},{18... | collective-permute-start | bytes 1179656 | tf_op jit(solution)/shard_map/ppermute | solution.py:159
  55.8 17.8 %collective-permute-start.14 = (bf16[3,256,256]{2,1,0:T(8,128)(2,1)S(1)}, bf16[3,256,256]{2,1,0:T(8,128)(2,1)S(1)}, u32[]{:S(2)}, u32[]{:S(2)}) collective-permute-start(bf16[3,256,256]{2,1,0:T(8,128)(2,1)S(1)} %slice_bitcast_fusion.2.refs_0_), channel_id=1, source_target_pairs={{0,8},{8,16},{16,24},{24,0},{1,9},{9,17},{17,25},{25,1},{2,10},{10... | collective-permute-start | bytes 1179656 | tf_op jit(solution)/shard_map/ppermute | solution.py:158
  67.5 8.6 %copy-start.1 = (bf16[2,3,256,256]{3,2,1,0:T(8,128)(2,1)}, bf16[2,3,256,256]{3,2,1,0:T(8,128)(2,1)S(1)}, u32[]{:S(2)}) copy-start(bf16[2,3,256,256]{3,2,1,0:T(8,128)(2,1)S(1)} %pad_maximum_fusion.1.refs_2_) | copy-start | bytes 2359300
  67.6 8.5 %collective-permute-start.13 = (bf16[2,3,256,256]{3,2,1,0:T(8,128)(2,1)S(1)}, bf16[2,3,256,256]{3,2,1,0:T(8,128)(2,1)S(1)}, u32[]{:S(2)}, u32[]{:S(2)}) collective-permute-start(bf16[2,3,256,256]{3,2,1,0:T(8,128)(2,1)S(1)} %pad_maximum_fusion.1.refs_2_), channel_id=1, source_target_pairs={{0,1},{1,0},{2,3},{3,2},{4,5},{5,4},{6,7},{7,6},{8,9},{9,8},{10,11... | collective-permute-start | bytes 2359304 | tf_op jit(solution)/shard_map/ppermute | solution.py:182
  69.0 17.2 %copy-start.7 = (bf16[3,256,256]{2,1,0:T(8,128)(2,1)}, bf16[3,256,256]{2,1,0:T(8,128)(2,1)S(1)}, u32[]{:S(2)}) copy-start(bf16[3,256,256]{2,1,0:T(8,128)(2,1)S(1)} %collective-permute-done.15.refs_2_) | copy-start | bytes 1179652
  73.6 12.7 %copy-start.8 = (bf16[3,256,256]{2,1,0:T(8,128)(2,1)}, bf16[3,256,256]{2,1,0:T(8,128)(2,1)S(1)}, u32[]{:S(2)}) copy-start(bf16[3,256,256]{2,1,0:T(8,128)(2,1)S(1)} %collective-permute-done.14.refs_1_) | copy-start | bytes 1179652
  74.8 18.8 %collective-permute-start.16 = (bf16[3,256,256]{2,1,0:T(8,128)(2,1)S(1)}, bf16[3,256,256]{2,1,0:T(8,128)(2,1)S(1)}, u32[]{:S(2)}, u32[]{:S(2)}) collective-permute-start(bf16[3,256,256]{2,1,0:T(8,128)(2,1)S(1)} %select_select_fusion), channel_id=1, source_target_pairs={{0,16},{24,8},{16,24},{8,0},{1,17},{25,9},{17,25},{9,1},{2,18},{26... | collective-permute-start | bytes 1179656 | tf_op jit(solution)/shard_map/ppermute | solution.py:161
  76.1 0.9 copy-start.10
  93.6 0.7 copy-start.11

commit v2 on v0

v2 whole, which is shorter than its diff:
```python
import functools

import jax
import jax.numpy as jnp
from jax import lax
from jax.experimental import pallas as pl
from jax.experimental.pallas import tpu as pltpu
from jax.sharding import PartitionSpec as P

F32 = jnp.float32
BF16 = jnp.bfloat16
IN_VMEM = pl.BlockSpec(memory_space=pltpu.VMEM)
IN_SMEM = pl.BlockSpec(memory_space=pltpu.SMEM)
IN_PLACE = pl.BlockSpec(memory_space=pl.ANY)
PARAMS = pltpu.CompilerParams(vmem_limit_bytes=20 * 1024 * 1024)
SMALL = pl.CostEstimate(flops=1000, bytes_accessed=1000, transcendentals=0)
LARGE = pl.CostEstimate(flops=17_000_000_000, bytes_accessed=1000, transcendentals=0)


def near_core(array):
    return pltpu.with_memory_space_constraint(array, pltpu.VMEM)


def dot(a, b):
    return jnp.dot(a, b, preferred_element_type=F32)


def wide_dot(a, b):
    high = a.astype(BF16)
    low = (a - high.astype(F32)).astype(BF16)
    return dot(high, b) + dot(low, b)


def pick_kernel(count, index, *refs):
    pieces, out = refs[:-1], refs[-1]
    for r, piece in enumerate(pieces):

        @pl.when(index[r] < count)
        def _():
            for n in range(out.shape[0]):
                out[n, index[r]] = piece[0]


def pick(count, copies, index, pieces):
    tile = pieces[0].shape[1]
    return pl.pallas_call(
        functools.partial(pick_kernel, count),
        out_shape=pltpu.VMEM((copies, count, tile, tile), BF16),
        in_specs=[IN_SMEM] + [IN_VMEM] * len(pieces),
        out_specs=IN_VMEM,
        cost_estimate=SMALL,
        compiler_params=PARAMS,
    )(index, *map(near_core, pieces))


def choose_kernel(flag, near0, near1, far0, far1, out):
    for value, pair in ((1, (near0, near1)), (0, (far0, far1))):

        @pl.when(flag[0] == value)
        def _():
            for j, source in enumerate(pair):
                out[j] = source[...]


def choose(flag, near0, near1, far0, far1):
    return pl.pallas_call(
        choose_kernel,
        out_shape=pltpu.VMEM((2,) + near0.shape, BF16),
        in_specs=[IN_SMEM] + [IN_VMEM] * 4,
        out_specs=IN_VMEM,
        cost_estimate=SMALL,
        compiler_params=PARAMS,
    )(flag, *map(near_core, (near0, near1, far0, far1)))


def solver_kernel(panels, parts, slot, lower_inverse, upper_inverse, *refs):
    heads, out, top, wide = refs[:parts], refs[parts], refs[parts + 1], refs[parts + 2]
    tile = out.shape[0] // panels
    per = panels // parts
    for i in range(parts):
        for j in range(per):
            k = slot[i * per + j]
            for m in range(panels - 1):
                top[k, m] = heads[i][m] if per == 1 else heads[i][j, m]
    for k in range(panels):
        col = slice(k * tile, (k + 1) * tile)
        if k:
            upper = [dot(lower_inverse[m], top[k, m]).astype(BF16) for m in range(k)]
            sums = []
            for j in range(k):
                total = wide_dot(wide[j * tile : (j + 1) * tile, j * tile : (j + 1) * tile], upper[j])
                for m in range(j + 1, k):
                    total += wide_dot(wide[j * tile : (j + 1) * tile, m * tile : (m + 1) * tile], upper[m])
                sums.append(total)
            above = -wide_dot(jnp.concatenate(sums), upper_inverse[k])
            wide[: k * tile, col] = above
            out[: k * tile, col] = above.astype(BF16)
        wide[col, col] = upper_inverse[k].astype(F32)
        out[col, col] = upper_inverse[k]


def solver(panels, slot, lower_inverse, upper_inverse, heads):
    tile = lower_inverse.shape[1]
    size = panels * tile
    return pl.pallas_call(
        functools.partial(solver_kernel, panels, len(heads)),
        out_shape=pltpu.VMEM((size, size), BF16),
        in_specs=[IN_SMEM] + [IN_VMEM] * (2 + len(heads)),
        out_specs=IN_VMEM,
        scratch_shapes=[pltpu.VMEM((panels, panels - 1, tile, tile), BF16), pltpu.VMEM((size, size), F32)],
        cost_estimate=LARGE,
        compiler_params=PARAMS,
    )(slot, near_core(lower_inverse), near_core(upper_inverse), *map(near_core, heads))


def gather_kernel(panels, skip, parts, slot, first, *refs):
    columns, out = refs[:parts], refs[-1]
    tile = out.shape[1] // panels
    per = panels // parts
    for i in range(parts):
        for j in range(per):
            k = slot[i * per + j]
            across = pl.ds(pl.multiple_of(k * tile, tile), tile)
            for a in range(columns[i].shape[1]):
                live = first[skip + a, 0] <= k
                block = columns[i][j, a]
                out[a * tile : (a + 1) * tile, across] = jnp.where(live, block, jnp.zeros_like(block))


def gather(panels, skip, slot, first, columns):
    tile = columns[0].shape[2]
    return pl.pallas_call(
        functools.partial(gather_kernel, panels, skip, len(columns)),
        out_shape=pltpu.VMEM((columns[0].shape[1] * tile, panels * tile), BF16),
        in_specs=[IN_SMEM] * 2 + [IN_VMEM] * len(columns),
        out_specs=IN_VMEM,
        cost_estimate=SMALL,
        compiler_params=PARAMS,
    )(slot, first, *map(near_core, columns))


def solve_tile(index, mask, inverse, r, c, block):
    k = index[r]
    return jnp.where(mask[k, c] == 1, dot(inverse[k], block), 0.0).astype(BF16)


def band(index, r, tile):
    return pl.ds(pl.multiple_of(index[r] * tile, tile), tile)


def update_kernel(panels, skip, index, place, mask, inverse, solve, raw, held, *refs):
    pieces, out, lowers, upper, done, sem = refs[:-5], *refs[-5:]
    tile, local_rows, local_cols = held.shape[2], held.shape[0], held.shape[1]
    rows, arrays = local_rows - skip, len(pieces) // panels
    row_at, column_at = place[0], place[1]

    def copy_out(a, c):
        return pltpu.make_async_copy(done.at[a, c], out.at[a, c], sem.at[a, c])

    own = pl.ds(pl.multiple_of(jnp.minimum(row_at, panels - 1) * tile, tile), tile)
    for k in range(panels):
        lowers[:, k * tile : (k + 1) * tile] = dot(
            raw[:, : (k + 1) * tile], solve[: (k + 1) * tile, k * tile : (k + 1) * tile]
        ).astype(BF16)
    c = 0
    for n in range(arrays):
        for j in range(pieces[n].shape[0]):
            for r in range(panels):
                block = pieces[r * arrays + n][j]
                upper[c, band(index, r, tile), :] = solve_tile(index, mask, inverse, r, c, block)
            c += 1
    for c in range(local_cols):
        for a in range(rows):
            s = held[a + skip, c].astype(F32) - dot(lowers[a * tile : (a + 1) * tile, :], upper[c])
            done[a + skip, c] = s.astype(BF16)
        if c == 0:
            for k in range(panels):

                @pl.when(column_at == k)
                def _():
                    for a in range(rows):
                        done[a + skip, 0] = lowers[a * tile : (a + 1) * tile, k * tile : (k + 1) * tile]

        if skip:
            done[0, c] = upper[c, own, :]
        else:

            @pl.when(row_at < panels)
            def _():
                done[0, c] = upper[c, own, :]

        for a in range(local_rows):
            copy_out(a, c).start()
    for c in range(local_cols):
        for a in range(local_rows):
            copy_out(a, c).wait()


def update(panels, skip, index, place, mask, inverse, solve, raw, held, pieces):
    tile, rows, cols = held.shape[2], held.shape[0], held.shape[1]
    flat = [array for piece in pieces for array in piece]
    return pl.pallas_call(
        functools.partial(update_kernel, panels, skip),
        out_shape=jax.ShapeDtypeStruct(held.shape, BF16),
        in_specs=[IN_SMEM] * 3 + [IN_VMEM] * (4 + len(flat)),
        out_specs=IN_PLACE,
        scratch_shapes=[
            pltpu.VMEM(raw.shape, BF16),
            pltpu.VMEM((cols, panels * tile, tile), BF16),
            pltpu.VMEM(held.shape, BF16),
            pltpu.SemaphoreType.DMA((rows, cols)),
        ],
        cost_estimate=SMALL,
        compiler_params=PARAMS,
    )(index, place, mask, near_core(inverse), solve, raw, held, *map(near_core, flat))


def along_rows(block, pairs):
    return lax.ppermute(block, "prow", pairs)


def up(block):
    return along_rows(block, [(0, 1), (1, 2), (2, 3), (3, 0)])


def down(block):
    return along_rows(block, [(1, 0), (2, 1), (3, 2), (0, 3)])


def over(block):
    return along_rows(block, [(0, 2), (1, 3), (2, 0), (3, 1)])


def to_far(block):
    return lax.ppermute(block, "pcol", [(0, 4), (1, 5), (2, 6), (3, 7)])


def beside_near(block):
    return lax.ppermute(block, "pcol", [(0, 2), (2, 0), (1, 3), (3, 1)])


def beside_far(block):
    return lax.ppermute(block, "pcol", [(4, 6), (6, 4), (5, 7), (7, 5)])


def twin(block):
    return lax.ppermute(block, "pcol", [(i, i ^ 1) for i in range(8)])


def after(block, *others):
    return lax.optimization_barrier((block, *others))[0]


def local(small, matrix, lower_inverse, upper_inverse, row_first, col_mask):
    panels, tile = lower_inverse.shape[0], lower_inverse.shape[1]
    local_rows, local_cols = matrix.shape[0], matrix.shape[2]
    grid = matrix.reshape(local_rows, local_cols, tile, tile)
    mask = col_mask.reshape(panels, local_cols)
    row_at, column_at = lax.axis_index("prow"), lax.axis_index("pcol")
    place = jnp.stack([row_at, column_at]).astype(jnp.int32)
    natural = jnp.arange(panels, dtype=jnp.int32)
    if small:
        skip = 1
        near = (column_at < 4).astype(jnp.int32).reshape(1)
        index = jnp.mod(row_at + jnp.array([0, 3, 1, 2]), 4).astype(jnp.int32)
        slot = jnp.bitwise_xor(jnp.bitwise_and(column_at, 3), jnp.array([0, 2, 1, 3])).astype(jnp.int32)
        own0, own1, column = grid[0, :1], grid[0, 1:], grid[1:, 0]

        up0, down0, over0 = up(own0), down(own0), over(own0)
        far = to_far(column)
        own1 = after(own1, up0, down0, over0)
        up1, down1 = up(own1), down(own1)
        side = beside_near(after(column, up0, down0, over0))
        cross = beside_far(far)
        tops = pick(panels - 1, 4, index, [own0, up0, down0, over0])
        tops = lax.all_to_all(tops, "pcol", 0, 0, axis_index_groups=[[0, 2, 4, 6], [1, 3, 5, 7]], tiled=True)

        passed = jnp.where(row_at == 2, up1, jnp.where(row_at == 1, down1, own1))
        rest = along_rows(passed, [(0, 2), (3, 1), (2, 3), (1, 0)])
        heads = [tops[0], tops[1]]
        core = jnp.bitwise_and(column_at, 1)
        head_slot = jnp.bitwise_xor(core, jnp.array([0, 2, 1, 3])).astype(jnp.int32)
        solve = solver(panels, head_slot, lower_inverse, upper_inverse, [after(heads[0], rest), heads[1], twin(heads[0]), twin(heads[1])])
        mine = choose(near, column, side, far, after(cross, passed))
        columns = [mine, twin(mine)]
        pieces = [[own0, own1], [up0, up1], [down0, down1], [over0, rest]]
    else:
        skip, index, slot = 0, natural, natural
        rows = lax.all_gather(grid[0], "prow")[:panels]
        pieces = [[rows[k]] for k in range(panels)]
        columns = jnp.where(natural[:, None, None, None] == column_at, grid[None, :, 0], 0)
        columns = [lax.psum(columns, "pcol")]
        tops = pick(panels - 1, 1, index, [rows[k] for k in range(panels)])[0]
        heads = jnp.where(natural[:, None, None, None] == column_at, tops[None], 0)
        heads = lax.psum(heads, "pcol")
        solve = solver(panels, natural, lower_inverse, upper_inverse, [heads])
    held = pltpu.with_memory_space_constraint(grid, pltpu.VMEM)
    raw = gather(panels, skip, slot, row_first, columns)
    result = update(panels, skip, index, place, mask, lower_inverse, solve, raw, held, pieces)
    return result.reshape(matrix.shape)


def solution(mesh):
    small = mesh.shape["prow"] == 4 and mesh.shape["pcol"] == 8

    def step(matrix, lower_inverse, upper_inverse, row_first, col_mask):
        fits = small and lower_inverse.shape[0] == 4 and matrix.shape[0] > 2 and matrix.shape[2] > 2
        return jax.shard_map(
            functools.partial(local, fits),
            mesh=mesh,
            in_specs=(
                P(None, "prow", None, "pcol", None, None),
                P(),
                P(),
                P(None, "prow"),
                P(None, None, "pcol"),
            ),
            out_specs=P(None, "prow", None, "pcol", None, None),
            check_vma=False,
        )(matrix, lower_inverse, upper_inverse, row_first, col_mask)

    return step
```

time: 527 us -> 91.6 us (0.17); the launches traced: 518 us -> 89.9 us
  local copies, waits for them, and re-layouts: 210 us -> 9.85 us
  waiting for transfers between devices: 206 us -> 33.7 us
  loops' own time: 40.6 us -> 0 us
  matrix products: 27.5 us -> 0 us
  starting transfers between devices: 0.35 us -> 22.8 us
  Pallas kernels: 0 us -> 20.7 us
  other arithmetic: 19.9 us -> 2.34 us
  between operations: 13.4 us -> 0.44 us
    psum x5 -> x0, waiting for transfers between devices: 206 us -> none  [spread(): return lax.psum(block, axis)]
    squeeze x64 -> x4, local copies, waits for them, and re-layouts: 72.9 us -> 5.27 us  [the longest x3 3.23 us: local(): own0, own1, column = (grid[0, :1], grid[0, 1:], grid[1:, 0])]
    dynamic_update_slice x64 -> x0, local copies, waits for them, and re-layouts: 50.2 us -> none  [apply_update(): return lax.map(update_row, (block, lower_panel, row_live))]
    another operation x80 -> x0, loops' own time: 40.6 us -> none  [the longest x8 39.9 us: apply_update(): return lax.map(update_row, (block, lower_panel, row_live))]
    dynamic_slice x64 -> x0, local copies, waits for them, and re-layouts: 39.8 us -> none  [apply_update(): return lax.map(update_row, (block, lower_panel, row_live))]
    ppermute x0 -> x12, waiting for transfers between devices: none -> 33.7 us  [the longest x6 29.4 us: along_rows(): return lax.ppermute(block, 'prow', pairs)]
    dot_general x22 -> x0, matrix products: 27.5 us -> none  [the longest x20 23.4 us: update_row(): jnp.einsum('ab,jbc->jac', lower_tile, upper_panel, preferred_element_type...]
    pallas_call x0 -> x5, Pallas kernels: none -> 20.7 us  [the longest x1 11.5 us: update(): pl.pallas_call(functools.partial(update_kernel, panels, skip), out_shape=...]
  transfers between devices with their start and end apart: 5 -> 13, of which waited for: 5 -> 5; matrix products, arithmetic and copies ran while one was open for 22% -> 7% of each run, Pallas kernels for 0% -> 8%
where the time goes in v2:
time: 91.6 us; the launch traced here: 89.9 us
  waiting for transfers between devices  33.7 us (37%)
  starting transfers between devices  22.8 us (25%)
  Pallas kernels  20.7 us (23%)
  local copies, waits for them, and re-layouts  9.85 us (11%)
  other arithmetic  2.34 us (3%)
    ppermute x6, waiting for transfers between devices, along_rows(): return lax.ppermute(block, 'prow', pairs)  29.4 us
    pallas_call x1, Pallas kernels, update(): pl.pallas_call(functools.partial(update_kernel, panels, skip), out_shape=...  11.5 us
    ppermute x6, starting transfers between devices, along_rows(): return lax.ppermute(block, 'prow', pairs)  7.41 us
    ppermute x1, starting transfers between devices, to_far(): return lax.ppermute(block, 'pcol', [(0, 4), (1, 5), (2, 6), (3, 7)])  4.93 us
    unnamed x43, local copies, waits for them, and re-layouts  4.58 us
    all_to_all x1, starting transfers between devices, local(): lax.all_to_all(tops, 'pcol', 0, 0, axis_index_groups=[[0, 2, 4, 6], [1, 3...  4.36 us
    ppermute x1, waiting for transfers between devices, beside_near(): return lax.ppermute(block, 'pcol', [(0, 2), (2, 0), (1, 3), (3, 1)])  4.31 us
    ppermute x1, starting transfers between devices, beside_near(): return lax.ppermute(block, 'pcol', [(0, 2), (2, 0), (1, 3), (3, 1)])  3.87 us
  transfers between devices with their start and end apart: 13, of which 5 were waited for; matrix products, arithmetic and copies ran while one was open for 7% of the time, Pallas kernels for 8%

profile of v2, /device:TPU:0, one launch (start us, length us, event | category | flops | bytes accessed | tf_op | source)
XLA Modules:
  0.0 89.9 jit_solution(6601466780441765436)
XLA Ops:
  0.0 1.2 %slice_bitcast_fusion.near0 = bf16[7,256,256]{2,1,0:T(8,128)(2,1)S(1)} fusion(bf16[8,5,256,256]{3,2,1,0:T(8,128)(2,1)} %bitcast.18), kind=kLoop, calls=%fused_computation | loop fusion | bytes 1835008 | tf_op jit(solution)/shard_map/squeeze | solution.py:267
  1.3 4.9 %collective-permute-start.9 = (bf16[7,256,256]{2,1,0:T(8,128)(2,1)S(1)}, bf16[7,256,256]{2,1,0:T(8,128)(2,1)S(1)}, u32[]{:S(2)}, u32[]{:S(2)}) collective-permute-start(bf16[7,256,256]{2,1,0:T(8,128)(2,1)S(1)} %slice_bitcast_fusion.near0), channel_id=1, source_target_pairs={{0,4},{1,5},{2,6},{3,7},{8,12},{9,13},{10,14},{11,15},{16,20},{17,... | collective-permute-start | bytes 2752520 | tf_op jit(solution)/shard_map/ppermute | solution.py:235
  6.2 0.9 %slice_bitcast_fusion.4.refs_0_ = bf16[1,256,256]{2,1,0:T(8,128)(2,1)S(1)} fusion(bf16[8,5,256,256]{3,2,1,0:T(8,128)(2,1)} %bitcast.19), kind=kLoop, calls=%fused_computation.5 | loop fusion | bytes 262144 | tf_op jit(solution)/shard_map/squeeze | solution.py:267
  7.1 2.7 %collective-permute-start.2 = (bf16[1,256,256]{2,1,0:T(8,128)(2,1)S(1)}, bf16[1,256,256]{2,1,0:T(8,128)(2,1)S(1)}, u32[]{:S(2)}, u32[]{:S(2)}) collective-permute-start(bf16[1,256,256]{2,1,0:T(8,128)(2,1)S(1)} %slice_bitcast_fusion.4.refs_0_), channel_id=1, source_target_pairs={{0,16},{8,24},{16,0},{24,8},{1,17},{9,25},{17,1},{25,9},{2,18},{10... | collective-permute-start | bytes 393224 | tf_op jit(solution)/shard_map/ppermute | solution.py:219
  9.8 1.3 %collective-permute-start.1 = (bf16[1,256,256]{2,1,0:T(8,128)(2,1)S(1)}, bf16[1,256,256]{2,1,0:T(8,128)(2,1)S(1)}, u32[]{:S(2)}, u32[]{:S(2)}) collective-permute-start(bf16[1,256,256]{2,1,0:T(8,128)(2,1)S(1)} %slice_bitcast_fusion.4.refs_0_), channel_id=1, source_target_pairs={{8,0},{16,8},{24,16},{0,24},{9,1},{17,9},{25,17},{1,25},{10,2},{18... | collective-permute-start | bytes 393224 | tf_op jit(solution)/shard_map/ppermute | solution.py:219
  11.1 0.7 collective-permute-start
  11.8 0.7 and_select_fusion.index
  12.5 7.4 %collective-permute-done.2.refs_3_.refs_6_ = bf16[1,256,256]{2,1,0:T(8,128)(2,1)S(1)} collective-permute-done((bf16[1,256,256]{2,1,0:T(8,128)(2,1)S(1)}, bf16[1,256,256]{2,1,0:T(8,128)(2,1)S(1)}, u32[]{:S(2)}, u32[]{:S(2)}) %collective-permute-start.2) | collective-permute-done | bytes 131104 | tf_op jit(solution)/shard_map/ppermute | solution.py:219
  19.8 1.8 %shard_map.82 = bf16[4,3,256,256]{3,2,1,0:T(8,128)(2,1)} custom-call(s32[4]{0:T(128)S(1)} %and_select_fusion.index, bf16[1,256,256]{2,1,0:T(8,128)(2,1)S(1)} %slice_bitcast_fusion.4.refs_0_, bf16[1,256,256]{2,1,0:T(8,128)(2,1)S(1)} %collective-permute-done.refs_1_.refs_2_, bf16[1,256,256]{2,1,0:T(8,128)(2,1)S(1)} %collective-permute-done.1.refs_2_.refs_4_, ...), custom_call_target="tpu_custom_call" | custom-call | flops 1000 | bytes 1000 | tf_op jit(solution)/shard_map/pallas_call | solution.py:46
  21.7 4.4 %all-to-all-start = ((bf16[4,3,256,256]{3,2,1,0:T(8,128)(2,1)}), bf16[4,3,256,256]{3,2,1,0:T(8,128)(2,1)}, u32[]{:S(2)}, u32[]{:S(2)}) async-start(bf16[4,3,256,256]{3,2,1,0:T(8,128)(2,1)} %shard_map.82), calls=%async_computation | async-start | bytes 3145728 | tf_op jit(solution)/shard_map/all_to_all | solution.py:276
  26.0 1.1 %slice_bitcast_fusion.1.refs_1_ = bf16[4,256,256]{2,1,0:T(8,128)(2,1)S(1)} fusion(bf16[8,5,256,256]{3,2,1,0:T(8,128)(2,1)} %bitcast.20), kind=kLoop, calls=%fused_computation.1 | loop fusion | bytes 1048576 | tf_op jit(solution)/shard_map/squeeze | solution.py:267
  27.1 2.7 %collective-permute-start.4 = (bf16[4,256,256]{2,1,0:T(8,128)(2,1)S(1)}, bf16[4,256,256]{2,1,0:T(8,128)(2,1)S(1)}, u32[]{:S(2)}, u32[]{:S(2)}) collective-permute-start(bf16[4,256,256]{2,1,0:T(8,128)(2,1)S(1)} %slice_bitcast_fusion.1.refs_1_), channel_id=1, source_target_pairs={{8,0},{16,8},{24,16},{0,24},{9,1},{17,9},{25,17},{1,25},{10,2},{18... | collective-permute-start | bytes 1572872 | tf_op jit(solution)/shard_map/ppermute | solution.py:219
  29.9 1.6 %collective-permute-start.10 = (bf16[7,256,256]{2,1,0:T(8,128)(2,1)S(1)}, bf16[7,256,256]{2,1,0:T(8,128)(2,1)}, u32[]{:S(2)}, u32[]{:S(2)}) collective-permute-start(bf16[7,256,256]{2,1,0:T(8,128)(2,1)S(1)} %collective-permute-done.9.far0), channel_id=1, source_target_pairs={{4,6},{6,4},{5,7},{7,5},{12,14},{14,12},{13,15},{15,13},{20,22},{2... | collective-permute-start | bytes 2752520 | tf_op jit(solution)/shard_map/ppermute | solution.py:243
  31.5 3.9 %collective-permute-start.8 = (bf16[7,256,256]{2,1,0:T(8,128)(2,1)S(1)}, bf16[7,256,256]{2,1,0:T(8,128)(2,1)}, u32[]{:S(2)}, u32[]{:S(2)}) collective-permute-start(bf16[7,256,256]{2,1,0:T(8,128)(2,1)S(1)} %slice_bitcast_fusion.near0), channel_id=1, source_target_pairs={{0,2},{2,0},{1,3},{3,1},{8,10},{10,8},{9,11},{11,9},{16,18},{18,16... | collective-permute-start | bytes 2752520 | tf_op jit(solution)/shard_map/ppermute | solution.py:239
  35.3 6.9 %collective-permute-done.4.refs_5_ = bf16[4,256,256]{2,1,0:T(8,128)(2,1)S(1)} collective-permute-done((bf16[4,256,256]{2,1,0:T(8,128)(2,1)S(1)}, bf16[4,256,256]{2,1,0:T(8,128)(2,1)S(1)}, u32[]{:S(2)}, u32[]{:S(2)}) %collective-permute-start.4) | collective-permute-done | bytes 524320 | tf_op jit(solution)/shard_map/ppermute | solution.py:219
  42.2 13.7 %collective-permute-done.3.refs_3_ = bf16[4,256,256]{2,1,0:T(8,128)(2,1)S(1)} collective-permute-done((bf16[4,256,256]{2,1,0:T(8,128)(2,1)S(1)}, bf16[4,256,256]{2,1,0:T(8,128)(2,1)S(1)}, u32[]{:S(2)}, u32[]{:S(2)}) %collective-permute-start.3) | collective-permute-done | bytes 524320 | tf_op jit(solution)/shard_map/ppermute | solution.py:219
  55.9 0.9 %select_select_fusion = bf16[4,256,256]{2,1,0:T(8,128)(2,1)} fusion(bf16[4,256,256]{2,1,0:T(8,128)(2,1)S(1)} %collective-permute-done.3.refs_3_, bf16[4,256,256]{2,1,0:T(8,128)(2,1)S(1)} %collective-permute-done.4.refs_5_, bf16[4,256,256]{2,1,0:T(8,128)(2,1)S(1)} %slice_bitcast_fusion.1.refs_1_, pred[]{:T(512)S(6)} %eq.9, pred[]{:T(512)S(6)} %eq.8), kind=kLoop, calls=%fused_computation.2 | loop fusion | flops 524288 | bytes 2097154 | tf_op jit(solution)/shard_map/jit(_where)/select_n | solution.py:278
  56.9 2.0 %slice_bitcast_fusion.2 = (bf16[3,256,256]{2,1,0:T(8,128)(2,1)}, bf16[3,256,256]{2,1,0:T(8,128)(2,1)}) fusion(bf16[4,3,256,256]{3,2,1,0:T(8,128)(2,1)} %all-to-all-done), kind=kLoop, calls=%fused_computation.3 | loop fusion | bytes 1572864 | tf_op jit(solution)/shard_map/squeeze | solution.py:280
  58.9 0.5 collective-permute-start.6
  59.4 4.3 %collective-permute-done.8.near1 = bf16[7,256,256]{2,1,0:T(8,128)(2,1)} collective-permute-done((bf16[7,256,256]{2,1,0:T(8,128)(2,1)S(1)}, bf16[7,256,256]{2,1,0:T(8,128)(2,1)}, u32[]{:S(2)}, u32[]{:S(2)}) %collective-permute-start.8) | collective-permute-done | bytes 917536 | tf_op jit(solution)/shard_map/ppermute | solution.py:239
  63.7 1.2 %copy-done.1 = bf16[7,256,256]{2,1,0:T(8,128)(2,1)S(1)} copy-done((bf16[7,256,256]{2,1,0:T(8,128)(2,1)S(1)}, bf16[7,256,256]{2,1,0:T(8,128)(2,1)}, u32[]{:S(2)}) %copy-start.1) | copy-done | bytes 917528
  64.9 1.2 %copy-done.7 = bf16[7,256,256]{2,1,0:T(8,128)(2,1)S(1)} copy-done((bf16[7,256,256]{2,1,0:T(8,128)(2,1)S(1)}, bf16[7,256,256]{2,1,0:T(8,128)(2,1)}, u32[]{:S(2)}) %copy-start.7) | copy-done | bytes 917528
  66.1 1.7 %shard_map.84.refs_0_ = bf16[2,7,256,256]{3,2,1,0:T(8,128)(2,1)S(1)} custom-call(s32[1]{0:T(128)} %bitcast.8.flag, bf16[7,256,256]{2,1,0:T(8,128)(2,1)S(1)} %copy-done.1, bf16[7,256,256]{2,1,0:T(8,128)(2,1)} %collective-permute-done.8.near1, bf16[7,256,256]{2,1,0:T(8,128)(2,1)S(1)} %copy-done.7, bf16[7,256,256]{2,1,0:T(8,128)(2,1)} %collective-permute-done.10.far1), custom_call_target="tpu_custom_call" | custom-call | flops 1000 | bytes 1000 | tf_op jit(solution)/shard_map/pallas_call | solution.py:66
  67.8 0.1 pad_add_fusion.place
  67.9 0.1 copy.9.first
  68.0 0.7 broadcast_xor_fusion
  68.7 1.5 %collective-permute-done.5.refs_7_ = bf16[4,256,256]{2,1,0:T(8,128)(2,1)} collective-permute-done((bf16[4,256,256]{2,1,0:T(8,128)(2,1)}, bf16[4,256,256]{2,1,0:T(8,128)(2,1)}, u32[]{:S(2)}, u32[]{:S(2)}) %collective-permute-start.5) | collective-permute-done | bytes 524320 | tf_op jit(solution)/shard_map/ppermute | solution.py:219
  70.2 1.0 %copy-done.14 = bf16[4,256,256]{2,1,0:T(8,128)(2,1)S(1)} copy-done((bf16[4,256,256]{2,1,0:T(8,128)(2,1)S(1)}, bf16[4,256,256]{2,1,0:T(8,128)(2,1)}, u32[]{:S(2)}) %copy-start.14) | copy-done | bytes 524312
  71.2 1.0 %copy-done.17 = bf16[4,256,256]{2,1,0:T(8,128)(2,1)S(1)} copy-done((bf16[4,256,256]{2,1,0:T(8,128)(2,1)S(1)}, bf16[4,256,256]{2,1,0:T(8,128)(2,1)}, u32[]{:S(2)}) %copy-start.17) | copy-done | bytes 524312
  72.3 3.7 %shard_map.83.solve = bf16[1024,1024]{1,0:T(8,128)(2,1)S(1)} custom-call(s32[4]{0:T(128)S(1)} %get-tuple-element.16.slot, bf16[4,256,256]{2,1,0:T(8,128)(2,1)S(1)} %copy-done.14, bf16[4,256,256]{2,1,0:T(8,128)(2,1)S(1)} %copy-done.17, bf16[3,256,256]{2,1,0:T(8,128)(2,1)} %get-tuple-element.10.refs_0_, bf16[3,256,256]{2,1,0:T(8,128)(2,1)} %get-tuple-element.13.refs_1_, ...), custom_call_target="tpu_custom_call" | custom-call | flops 16999999488 | bytes 1000 | tf_op jit(solution)/shard_map/pallas_call | solution.py:105
  76.0 2.1 %shard_map.85.raw = bf16[1792,1024]{1,0:T(8,128)(2,1)S(1)} custom-call(s32[4]{0:T(128)S(1)} %get-tuple-element.15.slot, s32[8,1]{1,0:T(8,128)S(1)} %copy.9.first, bf16[2,7,256,256]{3,2,1,0:T(8,128)(2,1)S(1)} %shard_map.84.refs_0_, bf16[2,7,256,256]{3,2,1,0:T(8,128)(2,1)} %collective-permute-done.11.refs_1_), custom_call_target="tpu_custom_call" | custom-call | flops 1000 | bytes 1000 | tf_op jit(solution)/shard_map/pallas_call | solution.py:132
  78.3 11.5 %shard_map.86 = bf16[8,5,256,256]{3,2,1,0:T(8,128)(2,1)} custom-call(s32[4]{0:T(128)S(1)} %and_select_fusion.index, s32[2]{0:T(128)S(1)} %pad_add_fusion.place, s32[4,5]{1,0:T(4,128)S(1)} %bitcast.24, bf16[4,256,256]{2,1,0:T(8,128)(2,1)S(1)} %copy-done.15, bf16[1024,1024]{1,0:T(8,128)(2,1)S(1)} %shard_map.83.solve, bf16[1792,1024]{1,0:T(8,128)(2,1)S(1)} %shard_map.85.raw, ...), custom_call_target="tpu_custom_call" | custom-call | flops 1000 | bytes 1000 | tf_op jit(solution)/shard_map/pallas_call | solution.py:202
  (51 shorter events, 0.2 us)
Async XLA Ops:
  1.2 55.6 %copy-start = (bf16[7,256,256]{2,1,0:T(8,128)(2,1)}, bf16[7,256,256]{2,1,0:T(8,128)(2,1)S(1)}, u32[]{:S(2)}) copy-start(bf16[7,256,256]{2,1,0:T(8,128)(2,1)S(1)} %slice_bitcast_fusion.near0) | copy-start | bytes 2752516
  1.3 28.6 %collective-permute-start.9 = (bf16[7,256,256]{2,1,0:T(8,128)(2,1)S(1)}, bf16[7,256,256]{2,1,0:T(8,128)(2,1)S(1)}, u32[]{:S(2)}, u32[]{:S(2)}) collective-permute-start(bf16[7,256,256]{2,1,0:T(8,128)(2,1)S(1)} %slice_bitcast_fusion.near0), channel_id=1, source_target_pairs={{0,4},{1,5},{2,6},{3,7},{8,12},{9,13},{10,14},{11,15},{16,20},{17,... | collective-permute-start | bytes 2752520 | tf_op jit(solution)/shard_map/ppermute | solution.py:235
  7.1 12.7 %collective-permute-start.2 = (bf16[1,256,256]{2,1,0:T(8,128)(2,1)S(1)}, bf16[1,256,256]{2,1,0:T(8,128)(2,1)S(1)}, u32[]{:S(2)}, u32[]{:S(2)}) collective-permute-start(bf16[1,256,256]{2,1,0:T(8,128)(2,1)S(1)} %slice_bitcast_fusion.4.refs_0_), channel_id=1, source_target_pairs={{0,16},{8,24},{16,0},{24,8},{1,17},{9,25},{17,1},{25,9},{2,18},{10... | collective-permute-start | bytes 393224 | tf_op jit(solution)/shard_map/ppermute | solution.py:219
  9.8 10.1 %collective-permute-start.1 = (bf16[1,256,256]{2,1,0:T(8,128)(2,1)S(1)}, bf16[1,256,256]{2,1,0:T(8,128)(2,1)S(1)}, u32[]{:S(2)}, u32[]{:S(2)}) collective-permute-start(bf16[1,256,256]{2,1,0:T(8,128)(2,1)S(1)} %slice_bitcast_fusion.4.refs_0_), channel_id=1, source_target_pairs={{8,0},{16,8},{24,16},{0,24},{9,1},{17,9},{25,17},{1,25},{10,2},{18... | collective-permute-start | bytes 393224 | tf_op jit(solution)/shard_map/ppermute | solution.py:219
  11.1 8.7 %collective-permute-start = (bf16[1,256,256]{2,1,0:T(8,128)(2,1)S(1)}, bf16[1,256,256]{2,1,0:T(8,128)(2,1)S(1)}, u32[]{:S(2)}, u32[]{:S(2)}) collective-permute-start(bf16[1,256,256]{2,1,0:T(8,128)(2,1)S(1)} %slice_bitcast_fusion.4.refs_0_), channel_id=1, source_target_pairs={{0,8},{8,16},{16,24},{24,0},{1,9},{9,17},{17,25},{25,1},{2,10},{10... | collective-permute-start | bytes 393224 | tf_op jit(solution)/shard_map/ppermute | solution.py:219
  19.8 1.8 %copy-start.8 = (bf16[1,256,256]{2,1,0:T(8,128)(2,1)}, bf16[1,256,256]{2,1,0:T(8,128)(2,1)S(1)}, u32[]{:S(2)}) copy-start(bf16[1,256,256]{2,1,0:T(8,128)(2,1)S(1)} %collective-permute-done.2.refs_3_.refs_6_) | copy-start | bytes 393220
  19.8 1.8 %copy-start.10 = (bf16[1,256,256]{2,1,0:T(8,128)(2,1)}, bf16[1,256,256]{2,1,0:T(8,128)(2,1)S(1)}, u32[]{:S(2)}) copy-start(bf16[1,256,256]{2,1,0:T(8,128)(2,1)S(1)} %collective-permute-done.1.refs_2_.refs_4_) | copy-start | bytes 393220
  19.8 1.8 %copy-start.12 = (bf16[1,256,256]{2,1,0:T(8,128)(2,1)}, bf16[1,256,256]{2,1,0:T(8,128)(2,1)S(1)}, u32[]{:S(2)}) copy-start(bf16[1,256,256]{2,1,0:T(8,128)(2,1)S(1)} %collective-permute-done.refs_1_.refs_2_) | copy-start | bytes 393220
  21.7 35.2 %all-to-all-start = ((bf16[4,3,256,256]{3,2,1,0:T(8,128)(2,1)}), bf16[4,3,256,256]{3,2,1,0:T(8,128)(2,1)}, u32[]{:S(2)}, u32[]{:S(2)}) async-start(bf16[4,3,256,256]{3,2,1,0:T(8,128)(2,1)} %shard_map.82), calls=%async_computation | async-start | bytes 3145728 | tf_op jit(solution)/shard_map/all_to_all | solution.py:276
  27.1 15.1 %collective-permute-start.4 = (bf16[4,256,256]{2,1,0:T(8,128)(2,1)S(1)}, bf16[4,256,256]{2,1,0:T(8,128)(2,1)S(1)}, u32[]{:S(2)}, u32[]{:S(2)}) collective-permute-start(bf16[4,256,256]{2,1,0:T(8,128)(2,1)S(1)} %slice_bitcast_fusion.1.refs_1_), channel_id=1, source_target_pairs={{8,0},{16,8},{24,16},{0,24},{9,1},{17,9},{25,17},{1,25},{10,2},{18... | collective-permute-start | bytes 1572872 | tf_op jit(solution)/shard_map/ppermute | solution.py:219
  29.8 26.1 %collective-permute-start.3 = (bf16[4,256,256]{2,1,0:T(8,128)(2,1)S(1)}, bf16[4,256,256]{2,1,0:T(8,128)(2,1)S(1)}, u32[]{:S(2)}, u32[]{:S(2)}) collective-permute-start(bf16[4,256,256]{2,1,0:T(8,128)(2,1)S(1)} %slice_bitcast_fusion.1.refs_1_), channel_id=1, source_target_pairs={{0,8},{8,16},{16,24},{24,0},{1,9},{9,17},{17,25},{25,1},{2,10},{10... | collective-permute-start | bytes 1572872 | tf_op jit(solution)/shard_map/ppermute | solution.py:219
  29.9 33.9 %copy-start.6 = (bf16[7,256,256]{2,1,0:T(8,128)(2,1)}, bf16[7,256,256]{2,1,0:T(8,128)(2,1)S(1)}, u32[]{:S(2)}) copy-start(bf16[7,256,256]{2,1,0:T(8,128)(2,1)S(1)} %collective-permute-done.9.far0) | copy-start | bytes 2752516
  29.9 29.6 %collective-permute-start.10 = (bf16[7,256,256]{2,1,0:T(8,128)(2,1)S(1)}, bf16[7,256,256]{2,1,0:T(8,128)(2,1)}, u32[]{:S(2)}, u32[]{:S(2)}) collective-permute-start(bf16[7,256,256]{2,1,0:T(8,128)(2,1)S(1)} %collective-permute-done.9.far0), channel_id=1, source_target_pairs={{4,6},{6,4},{5,7},{7,5},{12,14},{14,12},{13,15},{15,13},{20,22},{2... | collective-permute-start | bytes 2752520 | tf_op jit(solution)/shard_map/ppermute | solution.py:243
  31.5 32.3 %collective-permute-start.8 = (bf16[7,256,256]{2,1,0:T(8,128)(2,1)S(1)}, bf16[7,256,256]{2,1,0:T(8,128)(2,1)}, u32[]{:S(2)}, u32[]{:S(2)}) collective-permute-start(bf16[7,256,256]{2,1,0:T(8,128)(2,1)S(1)} %slice_bitcast_fusion.near0), channel_id=1, source_target_pairs={{0,2},{2,0},{1,3},{3,1},{8,10},{10,8},{9,11},{11,9},{16,18},{18,16... | collective-permute-start | bytes 2752520 | tf_op jit(solution)/shard_map/ppermute | solution.py:239
  42.2 21.5 %copy-start.2 = (bf16[4,256,256]{2,1,0:T(8,128)(2,1)}, bf16[4,256,256]{2,1,0:T(8,128)(2,1)S(1)}, u32[]{:S(2)}) copy-start(bf16[4,256,256]{2,1,0:T(8,128)(2,1)S(1)} %collective-permute-done.4.refs_5_) | copy-start | bytes 1572868
  55.9 7.8 %copy-start.4 = (bf16[4,256,256]{2,1,0:T(8,128)(2,1)}, bf16[4,256,256]{2,1,0:T(8,128)(2,1)S(1)}, u32[]{:S(2)}) copy-start(bf16[4,256,256]{2,1,0:T(8,128)(2,1)S(1)} %collective-permute-done.3.refs_3_) | copy-start | bytes 1572868
  56.8 11.1 %copy-start.18 = (s32[8,1]{0,1:T(1,128)S(1)}, s32[8,1]{0,1:T(1,128)}, u32[]{:S(2)}) copy-start(s32[8,1]{0,1:T(1,128)} %param.11) | copy-start | bytes 100
  56.8 13.3 %collective-permute-start.5 = (bf16[4,256,256]{2,1,0:T(8,128)(2,1)}, bf16[4,256,256]{2,1,0:T(8,128)(2,1)}, u32[]{:S(2)}, u32[]{:S(2)}) collective-permute-start(bf16[4,256,256]{2,1,0:T(8,128)(2,1)} %select_select_fusion), channel_id=1, source_target_pairs={{0,16},{24,8},{16,24},{8,0},{1,17},{25,9},{17,25},{9,1},{2,18},{26... | collective-permute-start | bytes 1572872 | tf_op jit(solution)/shard_map/ppermute | solution.py:219
  58.9 11.3 %collective-permute-start.7 = (bf16[3,256,256]{2,1,0:T(8,128)(2,1)}, bf16[3,256,256]{2,1,0:T(8,128)(2,1)}, u32[]{:S(2)}, u32[]{:S(2)}) collective-permute-start(bf16[3,256,256]{2,1,0:T(8,128)(2,1)} %get-tuple-element.13.refs_1_), channel_id=1, source_target_pairs={{0,1},{1,0},{2,3},{3,2},{4,5},{5,4},{6,7},{7,6},{8,9},{9,8},{10,11... | collective-permute-start | bytes 1179656 | tf_op jit(solution)/shard_map/ppermute | solution.py:247
  58.9 11.3 %collective-permute-start.6 = (bf16[3,256,256]{2,1,0:T(8,128)(2,1)}, bf16[3,256,256]{2,1,0:T(8,128)(2,1)}, u32[]{:S(2)}, u32[]{:S(2)}) collective-permute-start(bf16[3,256,256]{2,1,0:T(8,128)(2,1)} %get-tuple-element.10.refs_0_), channel_id=1, source_target_pairs={{0,1},{1,0},{2,3},{3,2},{4,5},{5,4},{6,7},{7,6},{8,9},{9,8},{10,11... | collective-permute-start | bytes 1179656 | tf_op jit(solution)/shard_map/ppermute | solution.py:247
  63.7 1.2 %copy-start.1 = (bf16[7,256,256]{2,1,0:T(8,128)(2,1)S(1)}, bf16[7,256,256]{2,1,0:T(8,128)(2,1)}, u32[]{:S(2)}) copy-start(bf16[7,256,256]{2,1,0:T(8,128)(2,1)} %copy-done) | copy-start | bytes 2752516
  64.9 1.2 %copy-start.7 = (bf16[7,256,256]{2,1,0:T(8,128)(2,1)S(1)}, bf16[7,256,256]{2,1,0:T(8,128)(2,1)}, u32[]{:S(2)}) copy-start(bf16[7,256,256]{2,1,0:T(8,128)(2,1)} %copy-done.6) | copy-start | bytes 2752516
  66.1 12.1 %slice-start = ((s8[5242880]{0:T(1024)(128)(4,1)}), s8[1048576]{0:T(1024)(128)(4,1)S(1)}, s32[]{:S(2)}) async-start(s8[5242880]{0:T(1024)(128)(4,1)} %bitcast.21), calls=%async_computation.1 | async-start | bytes 2097152
  67.8 8.2 %collective-permute-start.11 = (bf16[2,7,256,256]{3,2,1,0:T(8,128)(2,1)S(1)}, bf16[2,7,256,256]{3,2,1,0:T(8,128)(2,1)}, u32[]{:S(2)}, u32[]{:S(2)}) collective-permute-start(bf16[2,7,256,256]{3,2,1,0:T(8,128)(2,1)S(1)} %shard_map.84.refs_0_), channel_id=1, source_target_pairs={{0,1},{1,0},{2,3},{3,2},{4,5},{5,4},{6,7},{7,6},{8,9},{9,8},{10,11... | collective-permute-start | bytes 5505032 | tf_op jit(solution)/shard_map/ppermute | solution.py:247
  72.3 5.9 %slice-start.1 = ((s8[5242880]{0:T(1024)(128)(4,1)}), s8[4194304]{0:T(1024)(128)(4,1)S(1)}, s32[]{:S(2)}) async-start(s8[5242880]{0:T(1024)(128)(4,1)} %bitcast.21), calls=%async_computation.2 | async-start | bytes 8388608
  76.0 2.2 %copy-start.3 = (bf16[4,256,256]{2,1,0:T(8,128)(2,1)S(1)}, bf16[4,256,256]{2,1,0:T(8,128)(2,1)}, u32[]{:S(2)}) copy-start(bf16[4,256,256]{2,1,0:T(8,128)(2,1)} %copy-done.2) | copy-start | bytes 1572868
  76.0 2.2 %copy-start.5 = (bf16[4,256,256]{2,1,0:T(8,128)(2,1)S(1)}, bf16[4,256,256]{2,1,0:T(8,128)(2,1)}, u32[]{:S(2)}) copy-start(bf16[4,256,256]{2,1,0:T(8,128)(2,1)} %copy-done.4) | copy-start | bytes 1572868
  76.0 2.2 %copy-start.9 = (bf16[1,256,256]{2,1,0:T(8,128)(2,1)S(1)}, bf16[1,256,256]{2,1,0:T(8,128)(2,1)}, u32[]{:S(2)}) copy-start(bf16[1,256,256]{2,1,0:T(8,128)(2,1)} %copy-done.8) | copy-start | bytes 393220
  76.0 2.2 %copy-start.11 = (bf16[1,256,256]{2,1,0:T(8,128)(2,1)S(1)}, bf16[1,256,256]{2,1,0:T(8,128)(2,1)}, u32[]{:S(2)}) copy-start(bf16[1,256,256]{2,1,0:T(8,128)(2,1)} %copy-done.10) | copy-start | bytes 393220
  76.0 2.2 %copy-start.13 = (bf16[1,256,256]{2,1,0:T(8,128)(2,1)S(1)}, bf16[1,256,256]{2,1,0:T(8,128)(2,1)}, u32[]{:S(2)}) copy-start(bf16[1,256,256]{2,1,0:T(8,128)(2,1)} %copy-done.12) | copy-start | bytes 393220
  76.0 2.2 %copy-start.15 = (bf16[4,256,256]{2,1,0:T(8,128)(2,1)S(1)}, bf16[4,256,256]{2,1,0:T(8,128)(2,1)}, u32[]{:S(2)}) copy-start(bf16[4,256,256]{2,1,0:T(8,128)(2,1)} %inverse.1) | copy-start | bytes 1572868
  76.0 2.2 %copy-start.16 = (s32[4,5,1]{1,2,0:T(1,128)S(1)}, s32[4,5,1]{1,2,0:T(1,128)}, u32[]{:S(2)}) copy-start(s32[4,5,1]{1,2,0:T(1,128)} %param.12) | copy-start | bytes 244
  (2 other events, 2.1 us)

commit v3 on v2

--- a/solution.py
+++ b/solution.py
@@ -281,7 +281,7 @@
         core = jnp.bitwise_and(column_at, 1)
         head_slot = jnp.bitwise_xor(core, jnp.array([0, 2, 1, 3])).astype(jnp.int32)
         solve = solver(panels, head_slot, lower_inverse, upper_inverse, [after(heads[0], rest), heads[1], twin(heads[0]), twin(heads[1])])
-        mine = choose(near, column, side, far, after(cross, passed))
+        mine = choose(near, column, side, far, cross)
         columns = [mine, twin(mine)]
         pieces = [[own0, own1], [up0, up1], [down0, down1], [over0, rest]]
     else:

time: 91.6 us -> 91.7 us (level)
  no operation moved by 1% of the time
where the time goes in v3:
time: 91.7 us; the launch traced here: 89.9 us
  waiting for transfers between devices  33.7 us (37%)
  starting transfers between devices  22.8 us (25%)
  Pallas kernels  20.8 us (23%)
  local copies, waits for them, and re-layouts  9.88 us (11%)
  other arithmetic  2.34 us (3%)
    ppermute x6, waiting for transfers between devices, along_rows(): return lax.ppermute(block, 'prow', pairs)  29.4 us
    pallas_call x1, Pallas kernels, update(): pl.pallas_call(functools.partial(update_kernel, panels, skip), out_shape=...  11.5 us
    ppermute x6, starting transfers between devices, along_rows(): return lax.ppermute(block, 'prow', pairs)  7.41 us
    ppermute x1, starting transfers between devices, to_far(): return lax.ppermute(block, 'pcol', [(0, 4), (1, 5), (2, 6), (3, 7)])  4.93 us
    unnamed x43, local copies, waits for them, and re-layouts  4.59 us
    all_to_all x1, starting transfers between devices, local(): lax.all_to_all(tops, 'pcol', 0, 0, axis_index_groups=[[0, 2, 4, 6], [1, 3...  4.37 us
    ppermute x1, waiting for transfers between devices, beside_near(): return lax.ppermute(block, 'pcol', [(0, 2), (2, 0), (1, 3), (3, 1)])  4.29 us
    ppermute x1, starting transfers between devices, beside_near(): return lax.ppermute(block, 'pcol', [(0, 2), (2, 0), (1, 3), (3, 1)])  3.87 us
  transfers between devices with their start and end apart: 13, of which 5 were waited for; matrix products, arithmetic and copies ran while one was open for 7% of the time, Pallas kernels for 8%

profile of v3, /device:TPU:0, one launch (start us, length us, event | category | flops | bytes accessed | tf_op | source)
XLA Modules:
  0.0 89.9 jit_solution(13613549520289267793)
XLA Ops:
  0.0 1.2 %slice_bitcast_fusion.near0 = bf16[7,256,256]{2,1,0:T(8,128)(2,1)S(1)} fusion(bf16[8,5,256,256]{3,2,1,0:T(8,128)(2,1)} %bitcast.18), kind=kLoop, calls=%fused_computation | loop fusion | bytes 1835008 | tf_op jit(solution)/shard_map/squeeze | solution.py:267
  1.3 4.9 %collective-permute-start.9 = (bf16[7,256,256]{2,1,0:T(8,128)(2,1)S(1)}, bf16[7,256,256]{2,1,0:T(8,128)(2,1)S(1)}, u32[]{:S(2)}, u32[]{:S(2)}) collective-permute-start(bf16[7,256,256]{2,1,0:T(8,128)(2,1)S(1)} %slice_bitcast_fusion.near0), channel_id=1, source_target_pairs={{0,4},{1,5},{2,6},{3,7},{8,12},{9,13},{10,14},{11,15},{16,20},{17,... | collective-permute-start | bytes 2752520 | tf_op jit(solution)/shard_map/ppermute | solution.py:235
  6.2 0.9 %slice_bitcast_fusion.4.refs_0_ = bf16[1,256,256]{2,1,0:T(8,128)(2,1)S(1)} fusion(bf16[8,5,256,256]{3,2,1,0:T(8,128)(2,1)} %bitcast.19), kind=kLoop, calls=%fused_computation.5 | loop fusion | bytes 262144 | tf_op jit(solution)/shard_map/squeeze | solution.py:267
  7.1 2.7 %collective-permute-start.2 = (bf16[1,256,256]{2,1,0:T(8,128)(2,1)S(1)}, bf16[1,256,256]{2,1,0:T(8,128)(2,1)S(1)}, u32[]{:S(2)}, u32[]{:S(2)}) collective-permute-start(bf16[1,256,256]{2,1,0:T(8,128)(2,1)S(1)} %slice_bitcast_fusion.4.refs_0_), channel_id=1, source_target_pairs={{0,16},{8,24},{16,0},{24,8},{1,17},{9,25},{17,1},{25,9},{2,18},{10... | collective-permute-start | bytes 393224 | tf_op jit(solution)/shard_map/ppermute | solution.py:219
  9.8 1.3 %collective-permute-start.1 = (bf16[1,256,256]{2,1,0:T(8,128)(2,1)S(1)}, bf16[1,256,256]{2,1,0:T(8,128)(2,1)S(1)}, u32[]{:S(2)}, u32[]{:S(2)}) collective-permute-start(bf16[1,256,256]{2,1,0:T(8,128)(2,1)S(1)} %slice_bitcast_fusion.4.refs_0_), channel_id=1, source_target_pairs={{8,0},{16,8},{24,16},{0,24},{9,1},{17,9},{25,17},{1,25},{10,2},{18... | collective-permute-start | bytes 393224 | tf_op jit(solution)/shard_map/ppermute | solution.py:219
  11.1 0.7 collective-permute-start
  11.8 0.7 and_select_fusion.index
  12.5 7.4 %collective-permute-done.2.refs_3_.refs_6_ = bf16[1,256,256]{2,1,0:T(8,128)(2,1)S(1)} collective-permute-done((bf16[1,256,256]{2,1,0:T(8,128)(2,1)S(1)}, bf16[1,256,256]{2,1,0:T(8,128)(2,1)S(1)}, u32[]{:S(2)}, u32[]{:S(2)}) %collective-permute-start.2) | collective-permute-done | bytes 131104 | tf_op jit(solution)/shard_map/ppermute | solution.py:219
  19.8 1.8 %shard_map.82 = bf16[4,3,256,256]{3,2,1,0:T(8,128)(2,1)} custom-call(s32[4]{0:T(128)S(1)} %and_select_fusion.index, bf16[1,256,256]{2,1,0:T(8,128)(2,1)S(1)} %slice_bitcast_fusion.4.refs_0_, bf16[1,256,256]{2,1,0:T(8,128)(2,1)S(1)} %collective-permute-done.refs_1_.refs_2_, bf16[1,256,256]{2,1,0:T(8,128)(2,1)S(1)} %collective-permute-done.1.refs_2_.refs_4_, ...), custom_call_target="tpu_custom_call" | custom-call | flops 1000 | bytes 1000 | tf_op jit(solution)/shard_map/pallas_call | solution.py:46
  21.7 4.4 %all-to-all-start = ((bf16[4,3,256,256]{3,2,1,0:T(8,128)(2,1)}), bf16[4,3,256,256]{3,2,1,0:T(8,128)(2,1)}, u32[]{:S(2)}, u32[]{:S(2)}) async-start(bf16[4,3,256,256]{3,2,1,0:T(8,128)(2,1)} %shard_map.82), calls=%async_computation | async-start | bytes 3145728 | tf_op jit(solution)/shard_map/all_to_all | solution.py:276
  26.0 1.1 %slice_bitcast_fusion.1.refs_1_ = bf16[4,256,256]{2,1,0:T(8,128)(2,1)S(1)} fusion(bf16[8,5,256,256]{3,2,1,0:T(8,128)(2,1)} %bitcast.20), kind=kLoop, calls=%fused_computation.1 | loop fusion | bytes 1048576 | tf_op jit(solution)/shard_map/squeeze | solution.py:267
  27.1 2.7 %collective-permute-start.4 = (bf16[4,256,256]{2,1,0:T(8,128)(2,1)S(1)}, bf16[4,256,256]{2,1,0:T(8,128)(2,1)S(1)}, u32[]{:S(2)}, u32[]{:S(2)}) collective-permute-start(bf16[4,256,256]{2,1,0:T(8,128)(2,1)S(1)} %slice_bitcast_fusion.1.refs_1_), channel_id=1, source_target_pairs={{8,0},{16,8},{24,16},{0,24},{9,1},{17,9},{25,17},{1,25},{10,2},{18... | collective-permute-start | bytes 1572872 | tf_op jit(solution)/shard_map/ppermute | solution.py:219
  29.9 3.9 %collective-permute-start.8 = (bf16[7,256,256]{2,1,0:T(8,128)(2,1)S(1)}, bf16[7,256,256]{2,1,0:T(8,128)(2,1)}, u32[]{:S(2)}, u32[]{:S(2)}) collective-permute-start(bf16[7,256,256]{2,1,0:T(8,128)(2,1)S(1)} %slice_bitcast_fusion.near0), channel_id=1, source_target_pairs={{0,2},{2,0},{1,3},{3,1},{8,10},{10,8},{9,11},{11,9},{16,18},{18,16... | collective-permute-start | bytes 2752520 | tf_op jit(solution)/shard_map/ppermute | solution.py:239
  33.8 1.6 %collective-permute-start.10 = (bf16[7,256,256]{2,1,0:T(8,128)(2,1)S(1)}, bf16[7,256,256]{2,1,0:T(8,128)(2,1)}, u32[]{:S(2)}, u32[]{:S(2)}) collective-permute-start(bf16[7,256,256]{2,1,0:T(8,128)(2,1)S(1)} %collective-permute-done.9.far0), channel_id=1, source_target_pairs={{4,6},{6,4},{5,7},{7,5},{12,14},{14,12},{13,15},{15,13},{20,22},{2... | collective-permute-start | bytes 2752520 | tf_op jit(solution)/shard_map/ppermute | solution.py:243
  35.4 6.9 %collective-permute-done.4.refs_5_ = bf16[4,256,256]{2,1,0:T(8,128)(2,1)S(1)} collective-permute-done((bf16[4,256,256]{2,1,0:T(8,128)(2,1)S(1)}, bf16[4,256,256]{2,1,0:T(8,128)(2,1)S(1)}, u32[]{:S(2)}, u32[]{:S(2)}) %collective-permute-start.4) | collective-permute-done | bytes 524320 | tf_op jit(solution)/shard_map/ppermute | solution.py:219
  42.3 13.7 %collective-permute-done.3.refs_3_ = bf16[4,256,256]{2,1,0:T(8,128)(2,1)S(1)} collective-permute-done((bf16[4,256,256]{2,1,0:T(8,128)(2,1)S(1)}, bf16[4,256,256]{2,1,0:T(8,128)(2,1)S(1)}, u32[]{:S(2)}, u32[]{:S(2)}) %collective-permute-start.3) | collective-permute-done | bytes 524320 | tf_op jit(solution)/shard_map/ppermute | solution.py:219
  55.9 0.9 %select_select_fusion = bf16[4,256,256]{2,1,0:T(8,128)(2,1)} fusion(bf16[4,256,256]{2,1,0:T(8,128)(2,1)S(1)} %collective-permute-done.3.refs_3_, bf16[4,256,256]{2,1,0:T(8,128)(2,1)S(1)} %collective-permute-done.4.refs_5_, bf16[4,256,256]{2,1,0:T(8,128)(2,1)S(1)} %slice_bitcast_fusion.1.refs_1_, pred[]{:T(512)S(6)} %eq.9, pred[]{:T(512)S(6)} %eq.8), kind=kLoop, calls=%fused_computation.2 | loop fusion | flops 524288 | bytes 2097154 | tf_op jit(solution)/shard_map/jit(_where)/select_n | solution.py:278
  56.9 2.1 %slice_bitcast_fusion.2 = (bf16[3,256,256]{2,1,0:T(8,128)(2,1)}, bf16[3,256,256]{2,1,0:T(8,128)(2,1)}) fusion(bf16[4,3,256,256]{3,2,1,0:T(8,128)(2,1)} %all-to-all-done), kind=kLoop, calls=%fused_computation.3 | loop fusion | bytes 1572864 | tf_op jit(solution)/shard_map/squeeze | solution.py:280
  58.9 0.5 collective-permute-start.6
  59.4 4.3 %collective-permute-done.8.near1 = bf16[7,256,256]{2,1,0:T(8,128)(2,1)} collective-permute-done((bf16[7,256,256]{2,1,0:T(8,128)(2,1)S(1)}, bf16[7,256,256]{2,1,0:T(8,128)(2,1)}, u32[]{:S(2)}, u32[]{:S(2)}) %collective-permute-start.8) | collective-permute-done | bytes 917536 | tf_op jit(solution)/shard_map/ppermute | solution.py:239
  63.8 1.2 %copy-done.1 = bf16[7,256,256]{2,1,0:T(8,128)(2,1)S(1)} copy-done((bf16[7,256,256]{2,1,0:T(8,128)(2,1)S(1)}, bf16[7,256,256]{2,1,0:T(8,128)(2,1)}, u32[]{:S(2)}) %copy-start.1) | copy-done | bytes 917528
  64.9 1.2 %copy-done.7 = bf16[7,256,256]{2,1,0:T(8,128)(2,1)S(1)} copy-done((bf16[7,256,256]{2,1,0:T(8,128)(2,1)S(1)}, bf16[7,256,256]{2,1,0:T(8,128)(2,1)}, u32[]{:S(2)}) %copy-start.7) | copy-done | bytes 917528
  66.1 1.7 %shard_map.84.refs_0_ = bf16[2,7,256,256]{3,2,1,0:T(8,128)(2,1)S(1)} custom-call(s32[1]{0:T(128)} %bitcast.8.flag, bf16[7,256,256]{2,1,0:T(8,128)(2,1)S(1)} %copy-done.1, bf16[7,256,256]{2,1,0:T(8,128)(2,1)} %collective-permute-done.8.near1, bf16[7,256,256]{2,1,0:T(8,128)(2,1)S(1)} %copy-done.7, bf16[7,256,256]{2,1,0:T(8,128)(2,1)} %collective-permute-done.10.far1), custom_call_target="tpu_custom_call" | custom-call | flops 1000 | bytes 1000 | tf_op jit(solution)/shard_map/pallas_call | solution.py:66
  67.9 0.1 pad_add_fusion.place
  67.9 0.1 copy.9.first
  68.0 0.7 broadcast_xor_fusion
  68.7 1.5 %collective-permute-done.5.refs_7_ = bf16[4,256,256]{2,1,0:T(8,128)(2,1)} collective-permute-done((bf16[4,256,256]{2,1,0:T(8,128)(2,1)}, bf16[4,256,256]{2,1,0:T(8,128)(2,1)}, u32[]{:S(2)}, u32[]{:S(2)}) %collective-permute-start.5) | collective-permute-done | bytes 524320 | tf_op jit(solution)/shard_map/ppermute | solution.py:219
  70.2 1.0 %copy-done.14 = bf16[4,256,256]{2,1,0:T(8,128)(2,1)S(1)} copy-done((bf16[4,256,256]{2,1,0:T(8,128)(2,1)S(1)}, bf16[4,256,256]{2,1,0:T(8,128)(2,1)}, u32[]{:S(2)}) %copy-start.14) | copy-done | bytes 524312
  71.2 1.0 %copy-done.17 = bf16[4,256,256]{2,1,0:T(8,128)(2,1)S(1)} copy-done((bf16[4,256,256]{2,1,0:T(8,128)(2,1)S(1)}, bf16[4,256,256]{2,1,0:T(8,128)(2,1)}, u32[]{:S(2)}) %copy-start.17) | copy-done | bytes 524312
  72.3 3.7 %shard_map.83.solve = bf16[1024,1024]{1,0:T(8,128)(2,1)S(1)} custom-call(s32[4]{0:T(128)S(1)} %get-tuple-element.14.slot, bf16[4,256,256]{2,1,0:T(8,128)(2,1)S(1)} %copy-done.14, bf16[4,256,256]{2,1,0:T(8,128)(2,1)S(1)} %copy-done.17, bf16[3,256,256]{2,1,0:T(8,128)(2,1)} %get-tuple-element.9.refs_0_, bf16[3,256,256]{2,1,0:T(8,128)(2,1)} %get-tuple-element.11.refs_1_, ...), custom_call_target="tpu_custom_call" | custom-call | flops 16999999488 | bytes 1000 | tf_op jit(solution)/shard_map/pallas_call | solution.py:105
  76.0 2.1 %shard_map.85.raw = bf16[1792,1024]{1,0:T(8,128)(2,1)S(1)} custom-call(s32[4]{0:T(128)S(1)} %get-tuple-element.13.slot, s32[8,1]{1,0:T(8,128)S(1)} %copy.9.first, bf16[2,7,256,256]{3,2,1,0:T(8,128)(2,1)S(1)} %shard_map.84.refs_0_, bf16[2,7,256,256]{3,2,1,0:T(8,128)(2,1)} %collective-permute-done.11.refs_1_), custom_call_target="tpu_custom_call" | custom-call | flops 1000 | bytes 1000 | tf_op jit(solution)/shard_map/pallas_call | solution.py:132
  78.3 11.5 %shard_map.86 = bf16[8,5,256,256]{3,2,1,0:T(8,128)(2,1)} custom-call(s32[4]{0:T(128)S(1)} %and_select_fusion.index, s32[2]{0:T(128)S(1)} %pad_add_fusion.place, s32[4,5]{1,0:T(4,128)S(1)} %bitcast.24, bf16[4,256,256]{2,1,0:T(8,128)(2,1)S(1)} %copy-done.15, bf16[1024,1024]{1,0:T(8,128)(2,1)S(1)} %shard_map.83.solve, bf16[1792,1024]{1,0:T(8,128)(2,1)S(1)} %shard_map.85.raw, ...), custom_call_target="tpu_custom_call" | custom-call | flops 1000 | bytes 1000 | tf_op jit(solution)/shard_map/pallas_call | solution.py:202
  (51 shorter events, 0.2 us)
Async XLA Ops:
  1.2 55.6 %copy-start = (bf16[7,256,256]{2,1,0:T(8,128)(2,1)}, bf16[7,256,256]{2,1,0:T(8,128)(2,1)S(1)}, u32[]{:S(2)}) copy-start(bf16[7,256,256]{2,1,0:T(8,128)(2,1)S(1)} %slice_bitcast_fusion.near0) | copy-start | bytes 2752516
  1.3 32.5 %collective-permute-start.9 = (bf16[7,256,256]{2,1,0:T(8,128)(2,1)S(1)}, bf16[7,256,256]{2,1,0:T(8,128)(2,1)S(1)}, u32[]{:S(2)}, u32[]{:S(2)}) collective-permute-start(bf16[7,256,256]{2,1,0:T(8,128)(2,1)S(1)} %slice_bitcast_fusion.near0), channel_id=1, source_target_pairs={{0,4},{1,5},{2,6},{3,7},{8,12},{9,13},{10,14},{11,15},{16,20},{17,... | collective-permute-start | bytes 2752520 | tf_op jit(solution)/shard_map/ppermute | solution.py:235
  7.1 12.7 %collective-permute-start.2 = (bf16[1,256,256]{2,1,0:T(8,128)(2,1)S(1)}, bf16[1,256,256]{2,1,0:T(8,128)(2,1)S(1)}, u32[]{:S(2)}, u32[]{:S(2)}) collective-permute-start(bf16[1,256,256]{2,1,0:T(8,128)(2,1)S(1)} %slice_bitcast_fusion.4.refs_0_), channel_id=1, source_target_pairs={{0,16},{8,24},{16,0},{24,8},{1,17},{9,25},{17,1},{25,9},{2,18},{10... | collective-permute-start | bytes 393224 | tf_op jit(solution)/shard_map/ppermute | solution.py:219
  9.8 10.1 %collective-permute-start.1 = (bf16[1,256,256]{2,1,0:T(8,128)(2,1)S(1)}, bf16[1,256,256]{2,1,0:T(8,128)(2,1)S(1)}, u32[]{:S(2)}, u32[]{:S(2)}) collective-permute-start(bf16[1,256,256]{2,1,0:T(8,128)(2,1)S(1)} %slice_bitcast_fusion.4.refs_0_), channel_id=1, source_target_pairs={{8,0},{16,8},{24,16},{0,24},{9,1},{17,9},{25,17},{1,25},{10,2},{18... | collective-permute-start | bytes 393224 | tf_op jit(solution)/shard_map/ppermute | solution.py:219
  11.1 8.7 %collective-permute-start = (bf16[1,256,256]{2,1,0:T(8,128)(2,1)S(1)}, bf16[1,256,256]{2,1,0:T(8,128)(2,1)S(1)}, u32[]{:S(2)}, u32[]{:S(2)}) collective-permute-start(bf16[1,256,256]{2,1,0:T(8,128)(2,1)S(1)} %slice_bitcast_fusion.4.refs_0_), channel_id=1, source_target_pairs={{0,8},{8,16},{16,24},{24,0},{1,9},{9,17},{17,25},{25,1},{2,10},{10... | collective-permute-start | bytes 393224 | tf_op jit(solution)/shard_map/ppermute | solution.py:219
  19.8 1.8 %copy-start.8 = (bf16[1,256,256]{2,1,0:T(8,128)(2,1)}, bf16[1,256,256]{2,1,0:T(8,128)(2,1)S(1)}, u32[]{:S(2)}) copy-start(bf16[1,256,256]{2,1,0:T(8,128)(2,1)S(1)} %collective-permute-done.2.refs_3_.refs_6_) | copy-start | bytes 393220
  19.8 1.8 %copy-start.10 = (bf16[1,256,256]{2,1,0:T(8,128)(2,1)}, bf16[1,256,256]{2,1,0:T(8,128)(2,1)S(1)}, u32[]{:S(2)}) copy-start(bf16[1,256,256]{2,1,0:T(8,128)(2,1)S(1)} %collective-permute-done.1.refs_2_.refs_4_) | copy-start | bytes 393220
  19.8 1.8 %copy-start.12 = (bf16[1,256,256]{2,1,0:T(8,128)(2,1)}, bf16[1,256,256]{2,1,0:T(8,128)(2,1)S(1)}, u32[]{:S(2)}) copy-start(bf16[1,256,256]{2,1,0:T(8,128)(2,1)S(1)} %collective-permute-done.refs_1_.refs_2_) | copy-start | bytes 393220
  21.7 35.2 %all-to-all-start = ((bf16[4,3,256,256]{3,2,1,0:T(8,128)(2,1)}), bf16[4,3,256,256]{3,2,1,0:T(8,128)(2,1)}, u32[]{:S(2)}, u32[]{:S(2)}) async-start(bf16[4,3,256,256]{3,2,1,0:T(8,128)(2,1)} %shard_map.82), calls=%async_computation | async-start | bytes 3145728 | tf_op jit(solution)/shard_map/all_to_all | solution.py:276
  27.1 15.1 %collective-permute-start.4 = (bf16[4,256,256]{2,1,0:T(8,128)(2,1)S(1)}, bf16[4,256,256]{2,1,0:T(8,128)(2,1)S(1)}, u32[]{:S(2)}, u32[]{:S(2)}) collective-permute-start(bf16[4,256,256]{2,1,0:T(8,128)(2,1)S(1)} %slice_bitcast_fusion.1.refs_1_), channel_id=1, source_target_pairs={{8,0},{16,8},{24,16},{0,24},{9,1},{17,9},{25,17},{1,25},{10,2},{18... | collective-permute-start | bytes 1572872 | tf_op jit(solution)/shard_map/ppermute | solution.py:219
  29.9 26.1 %collective-permute-start.3 = (bf16[4,256,256]{2,1,0:T(8,128)(2,1)S(1)}, bf16[4,256,256]{2,1,0:T(8,128)(2,1)S(1)}, u32[]{:S(2)}, u32[]{:S(2)}) collective-permute-start(bf16[4,256,256]{2,1,0:T(8,128)(2,1)S(1)} %slice_bitcast_fusion.1.refs_1_), channel_id=1, source_target_pairs={{0,8},{8,16},{16,24},{24,0},{1,9},{9,17},{17,25},{25,1},{2,10},{10... | collective-permute-start | bytes 1572872 | tf_op jit(solution)/shard_map/ppermute | solution.py:219
  29.9 33.9 %collective-permute-start.8 = (bf16[7,256,256]{2,1,0:T(8,128)(2,1)S(1)}, bf16[7,256,256]{2,1,0:T(8,128)(2,1)}, u32[]{:S(2)}, u32[]{:S(2)}) collective-permute-start(bf16[7,256,256]{2,1,0:T(8,128)(2,1)S(1)} %slice_bitcast_fusion.near0), channel_id=1, source_target_pairs={{0,2},{2,0},{1,3},{3,1},{8,10},{10,8},{9,11},{11,9},{16,18},{18,16... | collective-permute-start | bytes 2752520 | tf_op jit(solution)/shard_map/ppermute | solution.py:239
  33.7 30.0 %copy-start.6 = (bf16[7,256,256]{2,1,0:T(8,128)(2,1)}, bf16[7,256,256]{2,1,0:T(8,128)(2,1)S(1)}, u32[]{:S(2)}) copy-start(bf16[7,256,256]{2,1,0:T(8,128)(2,1)S(1)} %collective-permute-done.9.far0) | copy-start | bytes 2752516
  33.8 30.0 %collective-permute-start.10 = (bf16[7,256,256]{2,1,0:T(8,128)(2,1)S(1)}, bf16[7,256,256]{2,1,0:T(8,128)(2,1)}, u32[]{:S(2)}, u32[]{:S(2)}) collective-permute-start(bf16[7,256,256]{2,1,0:T(8,128)(2,1)S(1)} %collective-permute-done.9.far0), channel_id=1, source_target_pairs={{4,6},{6,4},{5,7},{7,5},{12,14},{14,12},{13,15},{15,13},{20,22},{2... | collective-permute-start | bytes 2752520 | tf_op jit(solution)/shard_map/ppermute | solution.py:243
  42.3 21.5 %copy-start.2 = (bf16[4,256,256]{2,1,0:T(8,128)(2,1)}, bf16[4,256,256]{2,1,0:T(8,128)(2,1)S(1)}, u32[]{:S(2)}) copy-start(bf16[4,256,256]{2,1,0:T(8,128)(2,1)S(1)} %collective-permute-done.4.refs_5_) | copy-start | bytes 1572868
  55.9 7.8 %copy-start.4 = (bf16[4,256,256]{2,1,0:T(8,128)(2,1)}, bf16[4,256,256]{2,1,0:T(8,128)(2,1)S(1)}, u32[]{:S(2)}) copy-start(bf16[4,256,256]{2,1,0:T(8,128)(2,1)S(1)} %collective-permute-done.3.refs_3_) | copy-start | bytes 1572868
  56.9 11.1 %copy-start.18 = (s32[8,1]{0,1:T(1,128)S(1)}, s32[8,1]{0,1:T(1,128)}, u32[]{:S(2)}) copy-start(s32[8,1]{0,1:T(1,128)} %param.11) | copy-start | bytes 100
  56.9 13.3 %collective-permute-start.5 = (bf16[4,256,256]{2,1,0:T(8,128)(2,1)}, bf16[4,256,256]{2,1,0:T(8,128)(2,1)}, u32[]{:S(2)}, u32[]{:S(2)}) collective-permute-start(bf16[4,256,256]{2,1,0:T(8,128)(2,1)} %select_select_fusion), channel_id=1, source_target_pairs={{0,16},{24,8},{16,24},{8,0},{1,17},{25,9},{17,25},{9,1},{2,18},{26... | collective-permute-start | bytes 1572872 | tf_op jit(solution)/shard_map/ppermute | solution.py:219
  58.9 11.2 %collective-permute-start.7 = (bf16[3,256,256]{2,1,0:T(8,128)(2,1)}, bf16[3,256,256]{2,1,0:T(8,128)(2,1)}, u32[]{:S(2)}, u32[]{:S(2)}) collective-permute-start(bf16[3,256,256]{2,1,0:T(8,128)(2,1)} %get-tuple-element.11.refs_1_), channel_id=1, source_target_pairs={{0,1},{1,0},{2,3},{3,2},{4,5},{5,4},{6,7},{7,6},{8,9},{9,8},{10,11... | collective-permute-start | bytes 1179656 | tf_op jit(solution)/shard_map/ppermute | solution.py:247
  58.9 11.2 %collective-permute-start.6 = (bf16[3,256,256]{2,1,0:T(8,128)(2,1)}, bf16[3,256,256]{2,1,0:T(8,128)(2,1)}, u32[]{:S(2)}, u32[]{:S(2)}) collective-permute-start(bf16[3,256,256]{2,1,0:T(8,128)(2,1)} %get-tuple-element.9.refs_0_), channel_id=1, source_target_pairs={{0,1},{1,0},{2,3},{3,2},{4,5},{5,4},{6,7},{7,6},{8,9},{9,8},{10,11... | collective-permute-start | bytes 1179656 | tf_op jit(solution)/shard_map/ppermute | solution.py:247
  63.8 1.2 %copy-start.1 = (bf16[7,256,256]{2,1,0:T(8,128)(2,1)S(1)}, bf16[7,256,256]{2,1,0:T(8,128)(2,1)}, u32[]{:S(2)}) copy-start(bf16[7,256,256]{2,1,0:T(8,128)(2,1)} %copy-done) | copy-start | bytes 2752516
  64.9 1.2 %copy-start.7 = (bf16[7,256,256]{2,1,0:T(8,128)(2,1)S(1)}, bf16[7,256,256]{2,1,0:T(8,128)(2,1)}, u32[]{:S(2)}) copy-start(bf16[7,256,256]{2,1,0:T(8,128)(2,1)} %copy-done.6) | copy-start | bytes 2752516
  66.1 12.1 %slice-start = ((s8[5242880]{0:T(1024)(128)(4,1)}), s8[1048576]{0:T(1024)(128)(4,1)S(1)}, s32[]{:S(2)}) async-start(s8[5242880]{0:T(1024)(128)(4,1)} %bitcast.21), calls=%async_computation.1 | async-start | bytes 2097152
  67.8 8.2 %collective-permute-start.11 = (bf16[2,7,256,256]{3,2,1,0:T(8,128)(2,1)S(1)}, bf16[2,7,256,256]{3,2,1,0:T(8,128)(2,1)}, u32[]{:S(2)}, u32[]{:S(2)}) collective-permute-start(bf16[2,7,256,256]{3,2,1,0:T(8,128)(2,1)S(1)} %shard_map.84.refs_0_), channel_id=1, source_target_pairs={{0,1},{1,0},{2,3},{3,2},{4,5},{5,4},{6,7},{7,6},{8,9},{9,8},{10,11... | collective-permute-start | bytes 5505032 | tf_op jit(solution)/shard_map/ppermute | solution.py:247
  72.3 5.9 %slice-start.1 = ((s8[5242880]{0:T(1024)(128)(4,1)}), s8[4194304]{0:T(1024)(128)(4,1)S(1)}, s32[]{:S(2)}) async-start(s8[5242880]{0:T(1024)(128)(4,1)} %bitcast.21), calls=%async_computation.2 | async-start | bytes 8388608
  76.0 2.2 %copy-start.3 = (bf16[4,256,256]{2,1,0:T(8,128)(2,1)S(1)}, bf16[4,256,256]{2,1,0:T(8,128)(2,1)}, u32[]{:S(2)}) copy-start(bf16[4,256,256]{2,1,0:T(8,128)(2,1)} %copy-done.2) | copy-start | bytes 1572868
  76.0 2.2 %copy-start.5 = (bf16[4,256,256]{2,1,0:T(8,128)(2,1)S(1)}, bf16[4,256,256]{2,1,0:T(8,128)(2,1)}, u32[]{:S(2)}) copy-start(bf16[4,256,256]{2,1,0:T(8,128)(2,1)} %copy-done.4) | copy-start | bytes 1572868
  76.0 2.2 %copy-start.9 = (bf16[1,256,256]{2,1,0:T(8,128)(2,1)S(1)}, bf16[1,256,256]{2,1,0:T(8,128)(2,1)}, u32[]{:S(2)}) copy-start(bf16[1,256,256]{2,1,0:T(8,128)(2,1)} %copy-done.8) | copy-start | bytes 393220
  76.0 2.2 %copy-start.11 = (bf16[1,256,256]{2,1,0:T(8,128)(2,1)S(1)}, bf16[1,256,256]{2,1,0:T(8,128)(2,1)}, u32[]{:S(2)}) copy-start(bf16[1,256,256]{2,1,0:T(8,128)(2,1)} %copy-done.10) | copy-start | bytes 393220
  76.0 2.2 %copy-start.13 = (bf16[1,256,256]{2,1,0:T(8,128)(2,1)S(1)}, bf16[1,256,256]{2,1,0:T(8,128)(2,1)}, u32[]{:S(2)}) copy-start(bf16[1,256,256]{2,1,0:T(8,128)(2,1)} %copy-done.12) | copy-start | bytes 393220
  76.0 2.2 %copy-start.15 = (bf16[4,256,256]{2,1,0:T(8,128)(2,1)S(1)}, bf16[4,256,256]{2,1,0:T(8,128)(2,1)}, u32[]{:S(2)}) copy-start(bf16[4,256,256]{2,1,0:T(8,128)(2,1)} %inverse.1) | copy-start | bytes 1572868
  76.0 2.2 %copy-start.16 = (s32[4,5,1]{1,2,0:T(1,128)S(1)}, s32[4,5,1]{1,2,0:T(1,128)}, u32[]{:S(2)}) copy-start(s32[4,5,1]{1,2,0:T(1,128)} %param.12) | copy-start | bytes 244
  (2 other events, 2.1 us)
